TPU v7x, 128 devices: a whole 4x4x4 slice. The times are simulated.
128 devices in a mesh: inst: 16 (over z, x), tp: 8 (over y, core).
Axes of the slice: x: 4, y: 4, z: 4, core: 2. Of those that a mesh axis runs over, the one named last changes fastest.
Arguments:
- queries: bfloat16 [128, 4, 64, 128], P('inst', None, 'tp'), may hold values from -90 to 90
- tail_keys: bfloat16 [128, 8, 256, 128], P('inst', 'tp'), may hold values from -5 to 5
- tail_values: bfloat16 [128, 8, 256, 128], P('inst', 'tp'), may hold values from -6 to 6
- new_keys: bfloat16 [128, 4, 8, 128], P('inst', None, 'tp'), may hold values from -2.5 to 2.5
- new_values: bfloat16 [128, 4, 8, 128], P('inst', None, 'tp'), may hold values from -6 to 6
- tail_lengths: int32 [128], P('inst'), may hold values from 1 to 256
- pool_keys: bfloat16 [768, 8, 256, 128], P('inst', 'tp'), may hold values from -5 to 5
- pool_values: bfloat16 [768, 8, 256, 128], P('inst', 'tp'), may hold values from -6 to 6
- slot_request: int32 [768], P('inst'), may hold values from 0 to 127, as said below
- out_weight: bfloat16 [8192, 8192], P('tp'), may hold values from -0.0625 to 0.0625
Outputs:
- projected: bfloat16 [128, 4, 8192], P('inst', None, 'tp')
Inputs may be any that keep to these rules, and one draw needn't show every extreme that they name: `slot_request`: the 48 slots of one lender belong to 48 distinct requests; a request may have a slot on any lender or none.
All inputs are finite; a program needn't handle non-finite values.
Results may differ from a plain program's by a relative error of at most 0.019.
Values may be sent and summed in bfloat16 or wider, within the bound.
A program may use at most 128 MiB of HBM per device.

v0:
```python
import jax
import jax.numpy as jnp
from jax import lax
from jax.sharding import PartitionSpec as P

VERY_LOW = -1e30


def merged(value, axis, combine):
    everything = jax.tree.map(lambda part: lax.all_gather(part, axis), value)
    initial = jax.tree.map(lambda part: part[0], everything)

    def hop(k, so_far):
        return combine(so_far, jax.tree.map(lambda part: part[k], everything))

    return lax.fori_loop(1, lax.axis_size(axis), hop, initial)


def softmax_parts(scores):
    row_peak = jnp.max(scores, axis=-1)
    exp_terms = jnp.exp(scores - row_peak[..., None])
    exp_total = jnp.sum(exp_terms, axis=-1)
    return (row_peak, exp_terms.astype(jnp.bfloat16), exp_total)


def lender_partial(all_queries, pool_keys, pool_values, slot_request):
    request_count, step_count, head_count, head_size = all_queries.shape
    slot_count, kv_heads = (pool_keys.shape[0], pool_keys.shape[1])
    group_size = head_count // kv_heads
    query_rows = all_queries[slot_request].reshape(
        slot_count, step_count, kv_heads, group_size, head_size
    )
    scores = jnp.einsum(
        "psvgd,pvtd->psvgt", query_rows, pool_keys, preferred_element_type=jnp.float32
    ) * head_size ** (-0.5)
    row_peak, weights, exp_total = softmax_parts(scores)
    weighted_sum = jnp.einsum(
        "psvgt,pvtd->psvgd", weights, pool_values, preferred_element_type=jnp.float32
    )
    owner_mask = slot_request[None, :] == jnp.arange(request_count, dtype=jnp.int32)[:, None]
    best_peak = jnp.max(
        jnp.where(owner_mask[:, :, None, None, None], row_peak[None], VERY_LOW), axis=1
    )
    rescale = jnp.exp(row_peak - best_peak[slot_request])
    owner_matrix = owner_mask.astype(jnp.float32)
    denominator = jnp.dot(
        owner_matrix, (rescale * exp_total).reshape(slot_count, -1), precision=lax.Precision.HIGHEST
    ).reshape(best_peak.shape)
    numerator = jnp.dot(
        owner_matrix,
        (rescale[..., None] * weighted_sum).reshape(slot_count, -1),
        precision=lax.Precision.HIGHEST,
    ).reshape(best_peak.shape + (head_size,))
    has_block = (jnp.sum(owner_matrix, axis=1) > 0.5)[:, None, None, None]
    safe_total = jnp.where(has_block, denominator, 1.0)
    partial_out = jnp.where(has_block[..., None], numerator / safe_total[..., None], 0.0)
    log_total = jnp.where(has_block, best_peak + jnp.log(safe_total), VERY_LOW)
    return (
        partial_out.reshape(request_count, step_count, head_count, head_size),
        log_total.reshape(request_count, step_count, head_count),
    )


def local_partial(own_queries, tail_keys, tail_values, new_keys, new_values, tail_lengths):
    request_count, step_count, head_count, head_size = own_queries.shape
    kv_heads, block_len = (tail_keys.shape[1], tail_keys.shape[2])
    group_size = head_count // kv_heads
    query_rows = own_queries.reshape(request_count, step_count, kv_heads, group_size, head_size)
    old_scores = jnp.einsum(
        "rsvgd,rvtd->rsvgt", query_rows, tail_keys, preferred_element_type=jnp.float32
    )
    new_scores = jnp.einsum(
        "rsvgd,rjvd->rsvgj", query_rows, new_keys, preferred_element_type=jnp.float32
    )
    scores = jnp.concatenate([old_scores, new_scores], axis=-1) * head_size ** (-0.5)
    old_valid = jnp.arange(block_len, dtype=jnp.int32)[None, :] < tail_lengths[:, None]
    new_valid = (
        jnp.arange(step_count, dtype=jnp.int32)[None, :]
        <= jnp.arange(step_count, dtype=jnp.int32)[:, None]
    )
    old_valid = jnp.broadcast_to(old_valid[:, None, None, None, :], old_scores.shape)
    new_valid = jnp.broadcast_to(new_valid[None, :, None, None, :], new_scores.shape)
    scores = jnp.where(jnp.concatenate([old_valid, new_valid], axis=-1), scores, VERY_LOW)
    row_peak, weights, exp_total = softmax_parts(scores)
    weighted_sum = jnp.einsum(
        "rsvgt,rvtd->rsvgd",
        weights[..., :block_len],
        tail_values,
        preferred_element_type=jnp.float32,
    )
    weighted_sum = weighted_sum + jnp.einsum(
        "rsvgj,rjvd->rsvgd",
        weights[..., block_len:],
        new_values,
        preferred_element_type=jnp.float32,
    )
    local_out = weighted_sum / exp_total[..., None]
    local_log = row_peak + jnp.log(exp_total)
    return (
        local_out.reshape(request_count, step_count, head_count, head_size),
        local_log.reshape(request_count, step_count, head_count),
    )


def combine_pairs(earlier_pair, later_pair):
    earlier_out, earlier_log = earlier_pair
    later_out, later_log = later_pair
    top_log = jnp.maximum(earlier_log, later_log)
    earlier_scale = jnp.exp(earlier_log - top_log)
    later_scale = jnp.exp(later_log - top_log)
    scale_total = earlier_scale + later_scale
    merged_out = (
        earlier_out * earlier_scale[..., None] + later_out * later_scale[..., None]
    ) / scale_total[..., None]
    return (merged_out, top_log + jnp.log(scale_total))


def per_device(
    queries,
    tail_keys,
    tail_values,
    new_keys,
    new_values,
    tail_lengths,
    pool_keys,
    pool_values,
    slot_request,
    out_weight,
):
    own_count, step_count, head_count, head_size = queries.shape
    all_queries = lax.all_gather(queries, "inst", axis=0, tiled=True)
    partial_out, log_total = lender_partial(all_queries, pool_keys, pool_values, slot_request)
    local_out, local_log = local_partial(
        queries, tail_keys, tail_values, new_keys, new_values, tail_lengths
    )
    whole_out, whole_log = merged((partial_out, log_total), "inst", combine_pairs)
    first_row = lax.axis_index("inst") * own_count
    lent_out = lax.dynamic_slice_in_dim(whole_out, first_row, own_count, 0)
    lent_log = lax.dynamic_slice_in_dim(whole_log, first_row, own_count, 0)
    attention, _ = combine_pairs((local_out, local_log), (lent_out, lent_log))
    flat_rows = attention.astype(jnp.bfloat16).reshape(
        own_count * step_count, head_count * head_size
    )
    head_terms = jnp.dot(flat_rows, out_weight, preferred_element_type=jnp.float32).reshape(
        own_count, step_count, -1
    )
    return lax.psum_scatter(head_terms.astype(jnp.bfloat16), "tp", scatter_dimension=2, tiled=True)


def solution(mesh):
    placed = (
        P("inst", None, "tp", None),
        P("inst", "tp", None, None),
        P("inst", "tp", None, None),
        P("inst", None, "tp", None),
        P("inst", None, "tp", None),
        P("inst"),
        P("inst", "tp", None, None),
        P("inst", "tp", None, None),
        P("inst"),
        P("tp", None),
    )
    return jax.shard_map(
        per_device, mesh=mesh, in_specs=placed, out_specs=P("inst", None, "tp"), check_vma=False
    )
```

profile of v0, /device:TPU:1, one launch (start us, length us, event | category | flops | bytes accessed | tf_op | source)
XLA Modules:
  0.0 408.3 jit_solution(15105040446244941313)
XLA Ops:
  9.6 44.5 %all-gather.5.cloned.1.call-done = bf16[128,4,8,128]{3,2,1,0:T(8,128)(2,1)} async-done(((bf16[8,4,8,128]{3,2,1,0:T(8,128)(2,1)}), bf16[128,4,8,128]{3,2,1,0:T(8,128)(2,1)}) %all-gather.5.cloned.1.call-update) | async-done | bytes 1048592 | tf_op jit(solution)/shard_map/all_gather | solution.py:131
  54.1 1.8 gather_fusion
  61.0 3.1 fusion.25
  65.0 2.7 divide_select_fusion
  70.4 21.7 %all-gather.1 = f32[2048,4,8]{0,2,1:T(8,128)} all-gather(f32[128,4,8]{0,2,1:T(8,128)S(1)} %get-tuple-element.188), channel_id=3, replica_groups=mesh['inst'=16,'tp'=8] {'inst'}, dimensions={0}, use_global_device_ids=true | all-gather | bytes 278528 | tf_op jit(solution)/shard_map/all_gather | solution.py:10
  92.9 174.4 %all-gather.7.cloned.1.call-done = f32[2048,4,8,128]{3,0,2,1:T(8,128)} async-done(((f32[128,4,8,128]{3,0,2,1:T(8,128)}), f32[2048,4,8,128]{3,0,2,1:T(8,128)}) %all-gather.7.cloned.1.call-update) | async-done | bytes 33554448 | tf_op jit(solution)/shard_map/all_gather | solution.py:10
  270.1 90.4 %while.17 = (s32[]{:T(128)}, f32[128,4,8,128]{3,2,1,0:T(8,128)S(1)}, f32[128,4,8]{2,1,0:T(4,128)S(1)}, f32[16,128,4,8]{1,3,0,2:T(8,128)}, f32[16,128,4,8,128]{4,...) while((s32[]{:T(128)}, f32[128,4,8,128]{3,2,1,0:T(8,128)S(1)}, f32[128,4,8]{2,1,0:T(4,128)S(1)}, ...), condition=%wide.region_7.8_spmd, body=%wide.region_6.7_spmd.sunk | while | flops 2117637 | bytes 10698887 | solution.py:16
  273.0 3.1 fusion.65
  279.0 3.1 fusion.65
  285.1 3.1 fusion.65
  291.1 3.1 fusion.65
  297.1 3.1 fusion.65
  303.2 3.1 fusion.65
  309.2 3.1 fusion.65
  315.2 3.1 fusion.65
  321.2 3.1 fusion.65
  327.3 3.1 fusion.65
  333.3 3.1 fusion.65
  339.3 3.1 fusion.65
  345.3 3.1 fusion.65
  351.4 3.1 fusion.65
  357.4 3.1 fusion.65
  362.6 9.6 %fusion.6 = bf16[8,4,8192]{2,0,1:T(8,128)(2,1)} fusion(bf16[1024,8192]{1,0:T(8,128)(2,1)} %param.21, bf16[8,4,1024]{2,1,0:T(4,128)(2,1)S(1)} %dot_general.61), kind=kOutput, calls=%fused_computation.15 | convolution fusion | flops 537133056 | bytes 17367040 | tf_op jit(solution)/shard_map/dot_general | solution.py:144
  372.2 28.0 %reduce-scatter.2.cloned.1.call-done = bf16[8,4,1024]{2,0,1:T(8,128)(2,1)} async-done(((bf16[8,4,8192]{2,0,1:T(8,128)(2,1)}), bf16[8,4,1024]{2,0,1:T(8,128)(2,1)}) %reduce-scatter.2.cloned.1.call-update) | async-done | bytes 65552 | tf_op jit(solution)/shard_map/reduce_scatter | solution.py:147
  (121 shorter events, 61.9 us)
Async XLA Ops:
  6.5 49.4 %copy-start = (bf16[48,1,256,128]{3,2,1,0:T(8,128)(2,1)S(1)}, bf16[48,1,256,128]{3,2,1,0:T(8,128)(2,1)}, u32[]{:S(2)}) copy-start(bf16[48,1,256,128]{3,2,1,0:T(8,128)(2,1)} %param.18) | copy-start | bytes 9437188
  6.5 47.6 %all-gather.5.cloned.1.call-start = ((), (), s32[]{:S(2)}) async-start(), calls=%async_computation.1 | async-start | bytes 1114112 | tf_op jit(solution)/shard_map/all_gather | solution.py:131
  7.3 260.0 %all-gather.7.cloned.1.call-start = ((), (), s32[]{:S(2)}) async-start(), calls=%async_computation.3 | async-start | bytes 35651584 | tf_op jit(solution)/shard_map/all_gather | solution.py:10
  57.2 1.2 copy-start.2
  57.2 1.7 copy-start.3
  64.1 0.7 copy-start.9
  67.7 0.8 copy-start.4
  67.7 0.8 copy-start.7
  67.7 1.1 copy-start.5
  67.7 1.4 copy-start.10
  67.7 2.5 copy-start.8
  67.8 332.5 %reduce-scatter.2.cloned.1.call-start = ((), (), s32[]{:S(2)}) async-start(), calls=%async_computation.2 | async-start | bytes 589824 | tf_op jit(solution)/shard_map/reduce_scatter | solution.py:147
  70.2 197.1 %copy-start.6 = (bf16[8,4,1,8,260]{4,3,1,0,2:T(8,128)(2,1)}, bf16[8,4,1,8,260]{4,3,1,0,2:T(8,128)(2,1)S(1)}, u32[]{:S(2)}) copy-start(bf16[8,4,1,8,260]{4,3,1,0,2:T(8,128)(2,1)S(1)} %get-tuple-element.185) | copy-start | bytes 399364
  267.3 1.6 slice-start
  362.6 39.1 %copy-start.1 = (bf16[48,1,256,128]{3,2,1,0:T(8,128)(2,1)S(1)}, bf16[48,1,256,128]{3,2,1,0:T(8,128)(2,1)}, u32[]{:S(2)}) copy-start(bf16[48,1,256,128]{3,2,1,0:T(8,128)(2,1)} %param.18) | copy-start | bytes 9437188
Sparse Core Ops, SparseCore 0:
  9.5 44.5 all-gather.4
  67.9 199.3 all-gather.6
  372.3 27.8 reduce-scatter.1
where the time goes:
time: 412 us; the launch traced here: 408 us
  waiting for transfers between devices  248 us (60%)
  other arithmetic  56.6 us (14%)
  local copies, waits for them, and re-layouts  49.7 us (12%)
  blocking collectives  21.7 us (5%)
  matrix products  18.7 us (5%)
  between operations  13.3 us (3%)
    all_gather x1, waiting for transfers between devices, merged(): everything = jax.tree.map(lambda part: lax.all_gather(part, axis), value)  174 us
    div x15, other arithmetic, combine_pairs(): (earlier_out * earlier_scale[..., None] + later_out * later_scale[..., No...  46.6 us
    all_gather x1, waiting for transfers between devices, per_device(): all_queries = lax.all_gather(queries, 'inst', axis=0, tiled=True)  44.5 us
    dynamic_slice x45, local copies, waits for them, and re-layouts, hop(): return combine(so_far, jax.tree.map(lambda part: part[k], everything))  39.1 us
    reduce_scatter x1, waiting for transfers between devices, per_device(): lax.psum_scatter(head_terms.astype(jnp.bfloat16), 'tp', scatter_dimension...  28 us
    all_gather x1, blocking collectives, merged(): everything = jax.tree.map(lambda part: lax.all_gather(part, axis), value)  21.7 us
    dot_general x1, matrix products, per_device(): jnp.dot(flat_rows, out_weight, preferred_element_type=jnp.float32)  9.58 us
  transfers between devices with their start and end apart: 3, of which 3 were waited for; matrix products, arithmetic and copies ran while one was open for 1% of the time, Pallas kernels for 0%

commit v1 on v0

v1 whole, which is shorter than its diff:
```python
import functools

import jax
import jax.numpy as jnp
from jax import lax
from jax.experimental import pallas as pl
from jax.experimental.pallas import tpu as pltpu
from jax.sharding import PartitionSpec as P

MESH = pl.DeviceIdType.MESH
VERY_LOW = -1e30
HD = 128
LOG2E = 1.4426950408889634
SCALE2 = HD**-0.5 * LOG2E
NT = (((1,), (1,)), ((), ()))
F32, BF16, I32 = jnp.float32, jnp.bfloat16, jnp.int32

SLOTS = 48
OWN = 8
REQ = 128
ROWS = 32
STAGES = 1
R = ROWS // STAGES
PR = OWN * R // 8
GROUP = 12


def remote(src, dst, send_sem, recv_sem, device):
    return pltpu.make_async_remote_copy(
        src_ref=src, dst_ref=dst, send_sem=send_sem, recv_sem=recv_sem, device_id=device, device_id_type=MESH
    )


def iota(shape, dim):
    return lax.broadcasted_iota(I32, shape, dim)


def to_rows(one_hot, columns):
    copies = jnp.concatenate([columns] * (128 // R), axis=0)
    high = copies.astype(BF16)
    rest = copies - high.astype(F32)
    middle = rest.astype(BF16)
    low = (rest - middle.astype(F32)).astype(BF16)
    parts = [lax.dot_general(one_hot, part, NT, preferred_element_type=F32) for part in (high, middle, low)]
    return parts[0] + parts[1] + parts[2]


def scaled_sum(weight_row, parts):
    n = len(parts)
    lane, row = iota((R, 128), 1), iota((R, 128), 0)
    picked = jnp.where(lane % R == row, jnp.broadcast_to(weight_row, (R, 128)), 0.0).astype(BF16)
    stacked = jnp.concatenate(parts, axis=0) if n > 1 else parts[0]
    return jnp.dot(picked[:, : n * R], stacked, preferred_element_type=F32)


def merge_weights(logs):
    top = functools.reduce(jnp.maximum, logs)
    terms = [jnp.exp2(log - top) for log in logs]
    total = functools.reduce(jnp.add, terms)
    inverse = 1.0 / total
    return [term * inverse for term in terms], top + jnp.log2(total)


def by_lane_group(weights):
    group = iota(weights[0].shape, 1) // R
    result = weights[0]
    for k in range(1, len(weights)):
        result = jnp.where(group == k, weights[k], result)
    return result


def kernel(
    sr, tl, q_hbm, tk_hbm, tv_hbm, nk_hbm, nv_hbm, pk_hbm, pv_hbm, w_hbm,
    out,
    qall, qown, kb, vb, tkb, tvb, nkb, nvb, wb,
    po, omsg, lmsg, ro1, rl1, m1, l1, ro2, rl2, lo, lloc, att, cs, cr, ys, yr,
    rho, ivec, inv,
    lsem, qsem, gs, gr, s1, r1, s2, r2, css, crs, yss, yrs,
):
    inst, tp = lax.axis_index("inst"), lax.axis_index("tp")
    z, x, y, c = inst // 4, inst % 4, tp // 2, tp % 2

    def along(half, axis, k):
        if (axis == 0) == (half == 0):
            return {"inst": ((z + k) % 4) * 4 + x}
        return {"inst": z * 4 + (x + k) % 4}

    def place(half):
        return (z, x) if half == 0 else (x, z)

    def local_copy(i, src, dst):
        copy = pltpu.make_async_copy(src, dst, lsem.at[i])
        copy.start()
        return copy

    c_qown = local_copy(0, q_hbm, qown)
    c_tk, c_tv = local_copy(1, tk_hbm, tkb), local_copy(2, tv_hbm, tvb)
    c_nk, c_nv = local_copy(3, nk_hbm, nkb), local_copy(4, nv_hbm, nvb)
    c_k, c_v = local_copy(5, pk_hbm, kb), local_copy(6, pv_hbm, vb)

    barrier = pltpu.get_barrier_semaphore()
    peers = [along(0, axis, k) for axis in (0, 1) for k in (1, 2, 3)]
    peers += [{"tp": y * 2 + 1 - c}] + [{"tp": ((y + k) % 4) * 2 + c} for k in (1, 2, 3)]
    for peer in peers:
        pl.semaphore_signal(barrier, inc=1, device_id=peer, device_id_type=MESH)
    pl.semaphore_wait(barrier, len(peers))

    sent = []

    def send(src, dst, ss, rs, device):
        copy = remote(src, dst, ss, rs, device)
        copy.start()
        sent.append(copy)

    def chunk(half, dp, dq):
        p, q = place(half)
        return pl.ds(half * 64 + (((p + dp) % 4) * 4 + (q + dq) % 4) * 4, 4)

    own_copies = []
    for s in range(STAGES):
        for axis in (0, 1):
            for k in (2, 1, 3):
                for half in (0, 1):
                    back = (4 - k) % 4
                    sem = gr.at[s, half, back, 0] if axis == 0 else gr.at[s, half, 0, back]
                    send(
                        q_hbm.at[pl.ds(4 * half, 4), pl.ds(s * R, R)],
                        qall.at[s, chunk(half, 0, 0)],
                        gs.at[s, half, axis * 3 + k - 1],
                        sem,
                        along(half, axis, k),
                    )
        for half in (0, 1):
            copy = pltpu.make_async_copy(
                q_hbm.at[pl.ds(4 * half, 4), pl.ds(s * R, R)], qall.at[s, chunk(half, 0, 0)], qsem.at[s, half]
            )
            copy.start()
            own_copies.append(copy)
    c_w = local_copy(7, w_hbm, wb)

    def gathered(s, half, dp, dq):
        ref = qall.at[s, chunk(half, dp, dq)]
        remote(ref, ref, gs.at[s, half, 0], gr.at[s, half, dp, dq], along(half, 0, 1)).wait_recv()

    def forward(s):
        for dp in (3, 1, 2):
            for half in (0, 1):
                gathered(s, half, dp, 0)
                for k in (2, 1, 3):
                    ref = qall.at[s, chunk(half, dp, 0)]
                    send(ref, ref, gs.at[s, half, 3 + dp * 3 + k - 1], gr.at[s, half, dp, (4 - k) % 4], along(half, 1, k))

    lane8 = iota((8, 128), 1)
    at_slot = jnp.full((8, 128), -1, I32)
    slot_of = jnp.full((8, 128), SLOTS, I32)
    for j in range(SLOTS):
        request = sr[j]
        home, half, fourth = request // 8, (request % 8) // 4, request % 4
        swapped = (home % 4) * 4 + home // 4
        position = half * 64 + jnp.where(half == 0, home, swapped) * 4 + fourth
        rho[j] = position
        at_slot = jnp.where(lane8 == j, position, at_slot)
        slot_of = jnp.where(lane8 == position, j, slot_of)
    ivec[...] = slot_of
    c_inv = pltpu.make_async_copy(ivec, inv, lsem.at[8])
    c_inv.start()
    one_hot = (jnp.broadcast_to(at_slot[0:1], (REQ, 128)) == iota((REQ, 128), 0)).astype(F32)
    missing = (jnp.sum(one_hot, axis=1, keepdims=True) - 1.0) * (-VERY_LOW)
    one_hot = one_hot.astype(BF16)
    for s in range(STAGES):
        po[s, SLOTS] = jnp.zeros((R, HD), BF16)
    l1[...] = jnp.zeros_like(l1)
    lloc[...] = jnp.zeros_like(lloc)

    for s in range(STAGES):
        forward(s)

    c_qown.wait()
    c_tk.wait()
    c_tv.wait()
    c_nk.wait()
    c_nv.wait()
    new_scores = lax.dot_general(qown[...].reshape(OWN * ROWS, HD), nkb[...], NT, preferred_element_type=F32)
    token = iota((ROWS, 256), 1)
    new_lane, step = iota((ROWS, 32), 1), iota((ROWS, 32), 0) // 8
    lane, log_columns = iota((ROWS, 128), 1), jnp.zeros((ROWS, 128), F32)
    for r in range(OWN):
        old = lax.dot_general(qown[r], tkb[r], NT, preferred_element_type=F32)
        old = jnp.where(token < tl[r], old, VERY_LOW)
        new = new_scores[r * ROWS : (r + 1) * ROWS]
        new = jnp.where((new_lane >= 4 * r) & (new_lane <= 4 * r + step), new, VERY_LOW)
        peak = jnp.maximum(jnp.max(old, axis=1, keepdims=True), jnp.max(new, axis=1, keepdims=True))
        old = jnp.exp2((old - peak) * SCALE2)
        new = jnp.exp2((new - peak) * SCALE2)
        total = jnp.sum(old, axis=1, keepdims=True) + jnp.sum(new, axis=1, keepdims=True)
        result = jnp.dot(old.astype(BF16), tvb[r], preferred_element_type=F32)
        result = result + jnp.dot(new.astype(BF16), nvb[...], preferred_element_type=F32)
        lo[r] = (result * (1.0 / total)).astype(BF16)
        log_columns = jnp.where(lane == r, peak * SCALE2 + jnp.log2(total), log_columns)
    pick = (iota((OWN, 128), 0) == iota((OWN, 128), 1)).astype(F32).astype(BF16)
    for s in range(STAGES):
        rows = to_rows(pick, log_columns[s * R : (s + 1) * R])
        lloc[s, 0, 0:4] = rows[0:4]
        lloc[s, 1, 0:4] = rows[4:8]

    c_inv.wait()
    for copy in own_copies:
        copy.wait()

    def lend(s):
        lane = iota((R, 128), 1)

        def group(g, log_columns):
            scores = []
            for u in range(GROUP):
                j = g * GROUP + u
                scores.append(lax.dot_general(qall[s, rho[j]], kb[j], NT, preferred_element_type=F32))
            peaks = [jnp.max(score, axis=1, keepdims=True) for score in scores]
            terms = [jnp.exp2((score - peak) * SCALE2) for score, peak in zip(scores, peaks)]
            totals = [jnp.sum(term, axis=1, keepdims=True) for term in terms]
            for u in range(GROUP):
                j = g * GROUP + u
                result = jnp.dot(terms[u].astype(BF16), vb[j], preferred_element_type=F32)
                po[s, j] = (result * (1.0 / totals[u])).astype(BF16)
                log_columns = jnp.where(lane == j, peaks[u] * SCALE2 + jnp.log2(totals[u]), log_columns)
            return log_columns

        log_columns = lax.fori_loop(0, SLOTS // GROUP, group, jnp.zeros((R, 128), F32))
        lmsg[s] = to_rows(one_hot, log_columns) + missing

        def reorder(i, carry):
            for u in range(16):
                n = i * 16 + u
                omsg[s, n] = po[s, inv[0, n]]
            return carry

        lax.fori_loop(0, REQ // 16, reorder, 0)
        for k in (2, 1, 3):
            for half in (0, 1):
                p, _ = place(half)
                part = pl.ds(pl.multiple_of(half * 64 + ((p + k) % 4) * 16, 16), 16)
                to = along(half, 0, k)
                send(lmsg.at[s, part], rl1.at[s, half, k - 1], s1.at[s, half, k - 1, 0], r1.at[s, half, k - 1, 0], to)
                send(omsg.at[s, part], ro1.at[s, half, k - 1], s1.at[s, half, k - 1, 1], r1.at[s, half, k - 1, 1], to)

    def first_merge(s, half):
        p, q = place(half)
        base = pl.multiple_of(half * 64 + p * 16, 16)
        for k in (1, 3, 2):
            remote(rl1.at[s, half, k - 1], rl1.at[s, half, k - 1], s1.at[s, half, 0, 0], r1.at[s, half, k - 1, 0], along(half, 0, k)).wait_recv()
        logs = [lmsg[s, pl.ds(base, 16)]] + [rl1[s, half, k] for k in range(3)]
        weights, log = merge_weights(logs)
        weights = by_lane_group(weights)
        for i in range(4):
            l1[s, half, i, 0:4] = log[4 * i : 4 * i + 4]
        for k in (1, 3, 2):
            remote(ro1.at[s, half, k - 1], ro1.at[s, half, k - 1], s1.at[s, half, 0, 0], r1.at[s, half, k - 1, 1], along(half, 0, k)).wait_recv()
        for i in range(16):
            parts = [omsg[s, base + i]] + [ro1[s, half, k, i] for k in range(3)]
            m1[s, half, i] = scaled_sum(weights[i : i + 1], parts).astype(BF16)
        for k in (2, 1, 3):
            other = (q + k) % 4
            to = along(half, 1, k)
            send(l1.at[s, half, other], rl2.at[s, half, k - 1], s2.at[s, half, k - 1, 0], r2.at[s, half, k - 1, 0], to)
            send(m1.at[s, half, pl.ds(other * 4, 4)], ro2.at[s, half, k - 1], s2.at[s, half, k - 1, 1], r2.at[s, half, k - 1, 1], to)

    def second_merge(s, half):
        _, q = place(half)
        for k in (1, 3, 2):
            remote(rl2.at[s, half, k - 1], rl2.at[s, half, k - 1], s2.at[s, half, 0, 0], r2.at[s, half, k - 1, 0], along(half, 1, k)).wait_recv()
            remote(ro2.at[s, half, k - 1], ro2.at[s, half, k - 1], s2.at[s, half, 0, 0], r2.at[s, half, k - 1, 1], along(half, 1, k)).wait_recv()
        logs = [l1[s, half, q]] + [rl2[s, half, k] for k in range(3)] + [lloc[s, half]]
        weights, _ = merge_weights(logs)
        lent, home = by_lane_group(weights[:4]), weights[4]
        for i in range(4):
            parts = [m1[s, half, q * 4 + i]] + [ro2[s, half, k, i] for k in range(3)]
            r = half * 4 + i
            result = scaled_sum(lent[i : i + 1], parts)
            result = result + scaled_sum(home[i : i + 1], [lo[r, s * R : (s + 1) * R]])
            att[s, r * R : (r + 1) * R] = result

    def project(s):
        heads = [att[s, pl.ds(h, PR, stride=8)].astype(BF16) for h in range(8)]
        flat = jnp.concatenate(heads, axis=1)

        def columns(target):
            at = pl.multiple_of(target * 1024, 1024)
            return jnp.dot(flat, wb[:, pl.ds(at, 1024)], preferred_element_type=F32)

        for dy in (2, 1, 3, 0):
            cs[s, dy] = columns(((y + dy) % 4) * 2 + 1 - c).astype(BF16)
            send(cs.at[s, dy], cr.at[s, dy], css.at[s, dy], crs.at[s, dy], {"tp": y * 2 + 1 - c})
        mine = None
        for dy in (2, 1, 3, 0):
            value = columns(((y + dy) % 4) * 2 + c)
            remote(cr.at[s, dy], cr.at[s, dy], css.at[s, dy], crs.at[s, dy], {"tp": y * 2 + 1 - c}).wait_recv()
            value = value + cr[s, dy].astype(F32)
            if dy:
                ys[s, dy - 1] = value.astype(BF16)
                send(ys.at[s, dy - 1], yr.at[s, dy - 1], yss.at[s, dy - 1], yrs.at[s, dy - 1], {"tp": ((y + dy) % 4) * 2 + c})
            else:
                mine = value
        return mine

    def finish(s, value):
        for dy in (1, 3, 2):
            remote(yr.at[s, dy - 1], yr.at[s, dy - 1], yss.at[s, dy - 1], yrs.at[s, dy - 1], {"tp": ((y + dy) % 4) * 2 + c}).wait_recv()
            value = value + yr[s, dy - 1].astype(F32)
        out[s] = value.astype(BF16)

    for s in range(STAGES):
        for half in (0, 1):
            for dp in (0, 1, 3, 2):
                for dq in (1, 3, 2):
                    gathered(s, half, dp, dq)
        if s == 0:
            c_k.wait()
            c_v.wait()
        lend(s)
    for s in range(STAGES):
        for half in (0, 1):
            first_merge(s, half)
    for s in range(STAGES):
        for half in (0, 1):
            second_merge(s, half)
        if s == 0:
            c_w.wait()
        mine = project(s)
        finish(s, mine)
    for copy in sent:
        copy.wait_send()


def per_device(
    queries, tail_keys, tail_values, new_keys, new_values, tail_lengths, pool_keys, pool_values, slot_request, out_weight
):
    any_space = pl.BlockSpec(memory_space=pl.ANY)
    smem = pl.BlockSpec(memory_space=pltpu.SMEM)
    dma = pltpu.SemaphoreType.DMA
    S = STAGES

    def v(*shape, dtype=BF16):
        return pltpu.VMEM(shape, dtype)

    result = pl.pallas_call(
        kernel,
        out_shape=jax.ShapeDtypeStruct((S, PR, 1024), BF16),
        in_specs=[smem, smem] + [any_space] * 8,
        out_specs=pl.BlockSpec(memory_space=pltpu.VMEM),
        scratch_shapes=[
            v(S, REQ, R, HD), v(OWN, ROWS, HD), v(SLOTS, 256, HD), v(SLOTS, 256, HD), v(OWN, 256, HD), v(OWN, 256, HD),
            v(32, HD), v(32, HD), v(1024, 8192),
            v(S, SLOTS + 1, R, HD), v(S, REQ, R, HD), v(S, REQ, 128, dtype=F32),
            v(S, 2, 3, 16, R, HD), v(S, 2, 3, 16, 128, dtype=F32),
            v(S, 2, 16, R, HD), v(S, 2, 4, 8, 128, dtype=F32),
            v(S, 2, 3, 4, R, HD), v(S, 2, 3, 8, 128, dtype=F32),
            v(OWN, ROWS, HD), v(S, 2, 8, 128, dtype=F32), v(S, OWN * R, HD, dtype=F32),
            v(S, 4, PR, 1024), v(S, 4, PR, 1024), v(S, 3, PR, 1024), v(S, 3, PR, 1024),
            pltpu.SMEM((SLOTS,), I32), v(8, 128, dtype=I32), pltpu.SMEM((8, 128), I32),
            dma((9,)), dma((S, 2)), dma((S, 2, 15)), dma((S, 2, 4, 4)),
            dma((S, 2, 3, 2)), dma((S, 2, 3, 2)), dma((S, 2, 3, 2)), dma((S, 2, 3, 2)),
            dma((S, 4)), dma((S, 4)), dma((S, 3)), dma((S, 3)),
        ],
        name="lent_attention",
        compiler_params=pltpu.CompilerParams(collective_id=0, has_side_effects=True, vmem_limit_bytes=50 * 2**20),
    )(
        slot_request,
        tail_lengths,
        queries.reshape(OWN, ROWS, HD),
        tail_keys.reshape(OWN, 256, HD),
        tail_values.reshape(OWN, 256, HD),
        new_keys.reshape(32, HD),
        new_values.reshape(32, HD),
        pool_keys.reshape(SLOTS, 256, HD),
        pool_values.reshape(SLOTS, 256, HD),
        out_weight,
    )
    result = result.reshape(S, OWN, 4 // S, 1024)
    return result.transpose(1, 0, 2, 3).reshape(OWN, 4, 1024)


def solution(mesh):
    placed = (
        P("inst", None, "tp", None),
        P("inst", "tp", None, None),
        P("inst", "tp", None, None),
        P("inst", None, "tp", None),
        P("inst", None, "tp", None),
        P("inst"),
        P("inst", "tp", None, None),
        P("inst", "tp", None, None),
        P("inst"),
        P("tp", None),
    )
    return jax.shard_map(
        per_device, mesh=mesh, in_specs=placed, out_specs=P("inst", None, "tp"), check_vma=False
    )
```

time: 412 us -> 48 us (0.12)
  waiting for transfers between devices: 248 us -> 0 us
  other arithmetic: 56.6 us -> 0 us
  local copies, waits for them, and re-layouts: 49.7 us -> 6.28 us
  Pallas kernels: 0 us -> 41.3 us
  blocking collectives: 21.7 us -> 0 us
  matrix products: 18.7 us -> 0 us
  between operations: 13.3 us -> 0.02 us
    all_gather x2 -> x0, waiting for transfers between devices: 219 us -> none  [the longest x1 174 us: merged(): everything = jax.tree.map(lambda part: lax.all_gather(part, axis), value)]
    div x15 -> x0, other arithmetic: 46.6 us -> none  [combine_pairs(): (earlier_out * earlier_scale[..., None] + later_out * later_scale[..., No...]
    pallas_call x0 -> x1, Pallas kernels: none -> 41.3 us  [per_device(): pl.pallas_call(kernel, out_shape=jax.ShapeDtypeStruct((S, PR, 1024), BF16...]
    dynamic_slice x45 -> x0, local copies, waits for them, and re-layouts: 39.1 us -> none  [hop(): return combine(so_far, jax.tree.map(lambda part: part[k], everything))]
    reduce_scatter x1 -> x0, waiting for transfers between devices: 28 us -> none  [per_device(): lax.psum_scatter(head_terms.astype(jnp.bfloat16), 'tp', scatter_dimension...]
    all_gather x1 -> x0, blocking collectives: 21.7 us -> none  [merged(): everything = jax.tree.map(lambda part: lax.all_gather(part, axis), value)]
    dot_general x9 -> x0, matrix products: 18.7 us -> none  [the longest x1 9.58 us: per_device(): jnp.dot(flat_rows, out_weight, preferred_element_type=jnp.float32)]
    add x16 -> x0, other arithmetic: 4.77 us -> none  [the longest x15 4.02 us: combine_pairs(): return (merged_out, top_log + jnp.log(scale_total))]
  transfers between devices with their start and end apart: 3 -> 0, of which waited for: 3 -> 0; matrix products, arithmetic and copies ran while one was open for 1% -> 0% of each run, Pallas kernels for 0% -> 0%
where the time goes in v1:
time: 48 us; the launch traced here: 47.6 us
  Pallas kernels  41.3 us (86%)
  local copies, waits for them, and re-layouts  6.28 us (13%)
    pallas_call x1, Pallas kernels, per_device(): pl.pallas_call(kernel, out_shape=jax.ShapeDtypeStruct((S, PR, 1024), BF16...  41.3 us
    unnamed x14, local copies, waits for them, and re-layouts  5.62 us

profile of v1, /device:TPU:1, one launch (start us, length us, event | category | flops | bytes accessed | tf_op | source)
XLA Modules:
  0.0 47.6 jit_solution(1414176248299177454)
XLA Ops:
  0.0 0.0 copy-start
  0.0 1.0 %copy-done = bf16[8,1,256,128]{3,2,1,0:T(8,128)(2,1)S(1)} copy-done((bf16[8,1,256,128]{3,2,1,0:T(8,128)(2,1)S(1)}, bf16[8,1,256,128]{3,2,1,0:T(8,128)(2,1)}, u32[]{:S(2)}) %copy-start) | copy-done | bytes 524312
  1.0 0.0 copy-start.1
  1.0 1.0 %copy-done.1 = bf16[8,1,256,128]{3,2,1,0:T(8,128)(2,1)S(1)} copy-done((bf16[8,1,256,128]{3,2,1,0:T(8,128)(2,1)S(1)}, bf16[8,1,256,128]{3,2,1,0:T(8,128)(2,1)}, u32[]{:S(2)}) %copy-start.1) | copy-done | bytes 524312
  2.1 0.0 copy-start.2
  2.1 0.8 %copy-done.2 = bf16[8,4,8,128]{3,2,1,0:T(8,128)(2,1)S(1)} copy-done((bf16[8,4,8,128]{3,2,1,0:T(8,128)(2,1)S(1)}, bf16[8,4,8,128]{3,2,1,0:T(8,128)(2,1)}, u32[]{:S(2)}) %copy-start.2) | copy-done | bytes 65560
  2.9 0.0 copy-start.3
  2.9 0.7 %copy-done.3 = bf16[8,4,1,128]{3,1,2,0:T(4,128)(2,1)S(1)} copy-done((bf16[8,4,1,128]{3,1,2,0:T(4,128)(2,1)S(1)}, bf16[8,4,1,128]{3,1,2,0:T(4,128)(2,1)}, u32[]{:S(2)}) %copy-start.3) | copy-done | bytes 8216
  3.6 0.0 copy-start.4
  3.6 0.7 %copy-done.4 = bf16[8,4,1,128]{3,1,2,0:T(4,128)(2,1)S(1)} copy-done((bf16[8,4,1,128]{3,1,2,0:T(4,128)(2,1)S(1)}, bf16[8,4,1,128]{3,1,2,0:T(4,128)(2,1)}, u32[]{:S(2)}) %copy-start.4) | copy-done | bytes 8216
  4.3 0.0 copy-start.5
  4.3 0.7 %copy-done.5 = s32[48]{0:T(128)S(1)} copy-done((s32[48]{0:T(128)S(1)}, s32[48]{0:T(128)}, u32[]{:S(2)}) %copy-start.5) | copy-done | bytes 216
  5.0 0.0 copy-start.6
  5.0 0.7 %copy-done.6 = s32[8]{0:T(128)S(1)} copy-done((s32[8]{0:T(128)S(1)}, s32[8]{0:T(128)}, u32[]{:S(2)}) %copy-start.6) | copy-done | bytes 56
  5.6 41.3 %lent_attention.1 = bf16[1,32,1024]{2,1,0:T(8,128)(2,1)S(1)} custom-call(s32[48]{0:T(128)S(1)} %copy-done.5, s32[8]{0:T(128)S(1)} %copy-done.6, bf16[8,32,128]{2,1,0:T(8,128)(2,1)S(1)} %bitcast.9, bf16[8,256,128]{2,1,0:T(8,128)(2,1)S(1)} %bitcast.7, bf16[8,256,128]{2,1,0:T(8,128)(2,1)S(1)} %bitcast.8, bf16[32,128]{1,0:T(8,128)(2,1)S(1)} %bitcast.10, ...), custom_call_target="tpu_custom_call" | custom-call | tf_op jit(solution)/shard_map/lent_attention/pallas_call | solution.py:345
  47.0 0.7 %reshape_transpose_reshape.3 = bf16[8,4,1024]{2,1,0:T(4,128)(2,1)} reshape(bf16[1,32,1024]{2,1,0:T(8,128)(2,1)S(1)} %lent_attention.1) | data formatting | bytes 131072 | tf_op jit(solution)/shard_map/reshape;transpose;reshape | solution.py:379
Async XLA Ops:
  0.0 1.0 %copy-start = (bf16[8,1,256,128]{3,2,1,0:T(8,128)(2,1)S(1)}, bf16[8,1,256,128]{3,2,1,0:T(8,128)(2,1)}, u32[]{:S(2)}) copy-start(bf16[8,1,256,128]{3,2,1,0:T(8,128)(2,1)} %param.11) | copy-start | bytes 1572868
  1.0 1.0 %copy-start.1 = (bf16[8,1,256,128]{3,2,1,0:T(8,128)(2,1)S(1)}, bf16[8,1,256,128]{3,2,1,0:T(8,128)(2,1)}, u32[]{:S(2)}) copy-start(bf16[8,1,256,128]{3,2,1,0:T(8,128)(2,1)} %param.12) | copy-start | bytes 1572868
  2.1 0.8 %copy-start.2 = (bf16[8,4,8,128]{3,2,1,0:T(8,128)(2,1)S(1)}, bf16[8,4,8,128]{3,2,1,0:T(8,128)(2,1)}, u32[]{:S(2)}) copy-start(bf16[8,4,8,128]{3,2,1,0:T(8,128)(2,1)} %param.10) | copy-start | bytes 196612
  2.9 0.7 %copy-start.3 = (bf16[8,4,1,128]{3,1,2,0:T(4,128)(2,1)S(1)}, bf16[8,4,1,128]{3,1,2,0:T(4,128)(2,1)}, u32[]{:S(2)}) copy-start(bf16[8,4,1,128]{3,1,2,0:T(4,128)(2,1)} %param.13) | copy-start | bytes 24580
  3.6 0.7 %copy-start.4 = (bf16[8,4,1,128]{3,1,2,0:T(4,128)(2,1)S(1)}, bf16[8,4,1,128]{3,1,2,0:T(4,128)(2,1)}, u32[]{:S(2)}) copy-start(bf16[8,4,1,128]{3,1,2,0:T(4,128)(2,1)} %param.14) | copy-start | bytes 24580
  4.3 0.7 %copy-start.5 = (s32[48]{0:T(128)S(1)}, s32[48]{0:T(128)}, u32[]{:S(2)}) copy-start(s32[48]{0:T(128)} %sr.1) | copy-start | bytes 580
  5.0 0.7 %copy-start.6 = (s32[8]{0:T(128)S(1)}, s32[8]{0:T(128)}, u32[]{:S(2)}) copy-start(s32[8]{0:T(128)} %tl.1) | copy-start | bytes 100

commit v2 on v1

v2 whole, which is shorter than its diff:
```python
import functools

import jax
import jax.numpy as jnp
from jax import lax
from jax.experimental import pallas as pl
from jax.experimental.pallas import tpu as pltpu
from jax.sharding import PartitionSpec as P

MESH = pl.DeviceIdType.MESH
VERY_LOW = -1e30
HD = 128
LOG2E = 1.4426950408889634
SCALE2 = HD**-0.5 * LOG2E
NT = (((1,), (1,)), ((), ()))
F32, BF16, I32 = jnp.float32, jnp.bfloat16, jnp.int32

SLOTS = 48
OWN = 8
REQ = 128
R = 32
PAIRS = 16
FORWARD = (2, 3, 1)
FIRST = (2, 1, 3)


def remote(src, dst, send_sem, recv_sem, device):
    return pltpu.make_async_remote_copy(
        src_ref=src, dst_ref=dst, send_sem=send_sem, recv_sem=recv_sem, device_id=device, device_id_type=MESH
    )


def iota(shape, dim):
    return lax.broadcasted_iota(I32, shape, dim)


def to_rows(one_hot, columns):
    copies = jnp.concatenate([columns] * (128 // R), axis=0)
    high = copies.astype(BF16)
    rest = copies - high.astype(F32)
    middle = rest.astype(BF16)
    low = (rest - middle.astype(F32)).astype(BF16)
    parts = [lax.dot_general(one_hot, part, NT, preferred_element_type=F32) for part in (high, middle, low)]
    return parts[0] + parts[1] + parts[2]


def scaled_sums(weights, parts):
    lane, row = iota((R, 128), 1), iota((R, 128), 0)
    diagonal = lane % R == row
    zeros = jnp.zeros((R, 128), BF16)
    picked = [jnp.where(diagonal, jnp.broadcast_to(weights[i : i + 1], (R, 128)), 0.0).astype(BF16) for i in range(4)]
    rows = [jnp.concatenate([zeros, pick] if i % 2 else [pick, zeros], axis=1) for i, pick in enumerate(picked)]
    left = jnp.concatenate(parts[0] + parts[1], axis=0)
    right = jnp.concatenate(parts[2] + parts[3], axis=0)
    result = jnp.dot(jnp.concatenate(rows, axis=0), jnp.concatenate([left, right], axis=1), preferred_element_type=F32)
    return [result[i * R : (i + 1) * R, (i // 2) * 128 : (i // 2 + 1) * 128] for i in range(4)]


def merge_weights(logs):
    top = functools.reduce(jnp.maximum, logs)
    terms = [jnp.exp2(log - top) for log in logs]
    total = functools.reduce(jnp.add, terms)
    inverse = 1.0 / total
    return [term * inverse for term in terms], top + jnp.log2(total)


def by_lane_group(weights):
    group = iota(weights[0].shape, 1) // R
    result = weights[0]
    for k in range(1, len(weights)):
        result = jnp.where(group == k, weights[k], result)
    return result


def kernel(
    sr_hbm, tl_hbm, q_hbm, tk_hbm, tv_hbm, nk_hbm, nv_hbm, pk_hbm, pv_hbm, w_hbm,
    out,
    qall, qown, kb, vb, tkb, tvb, nkb, nvb, wb,
    omsg, lmsg, absent, ro1, rl1, m1, l1, ro2, rl2, lo, lloc, att, cs, cr, ys, yr,
    sr, tl, ivec, inv,
    lsem, qsem, gs, gr, s1, r1, s2, r2, css, crs, yss, yrs,
):
    inst, tp = lax.axis_index("inst"), lax.axis_index("tp")
    z, x, y, c = inst // 4, inst % 4, tp // 2, tp % 2

    def along(half, axis, k):
        if (axis == 0) == (half == 0):
            return {"inst": ((z + k) % 4) * 4 + x}
        return {"inst": z * 4 + (x + k) % 4}

    def place(half):
        return (z, x) if half == 0 else (x, z)

    barrier = pltpu.get_barrier_semaphore()
    peers = [along(0, axis, k) for axis in (0, 1) for k in (2, 1, 3)]
    peers += [{"tp": ((y + k) % 4) * 2 + c} for k in (2, 1, 3)] + [{"tp": y * 2 + 1 - c}]
    for peer in peers:
        pl.semaphore_signal(barrier, inc=1, device_id=peer, device_id_type=MESH)

    def local_copy(i, src, dst):
        copy = pltpu.make_async_copy(src, dst, lsem.at[i])
        copy.start()
        return copy

    c_sr, c_tl = local_copy(9, sr_hbm, sr), local_copy(10, tl_hbm, tl)
    c_qown = local_copy(0, q_hbm, qown)
    c_k, c_v = local_copy(5, pk_hbm, kb), local_copy(6, pv_hbm, vb)
    pl.semaphore_wait(barrier, len(peers))

    sent = []

    def send(src, dst, ss, rs, device):
        copy = remote(src, dst, ss, rs, device)
        copy.start()
        sent.append(copy)

    def received(dst, ss, rs):
        remote(dst, dst, ss, rs, along(0, 0, 1)).wait_recv()

    def chunk(half, dp, dq):
        p, q = place(half)
        return pl.ds(half * 64 + (((p + dp) % 4) * 4 + (q + dq) % 4) * 4, 4)

    for axis in (0, 1):
        for k in (2, 1, 3):
            for half in (0, 1):
                back = (4 - k) % 4
                send(
                    q_hbm.at[pl.ds(4 * half, 4)],
                    qall.at[chunk(half, 0, 0)],
                    gs.at[half, axis * 3 + k - 1],
                    gr.at[half, back, 0] if axis == 0 else gr.at[half, 0, back],
                    along(half, axis, k),
                )
    own_copies = []
    for half in (0, 1):
        copy = pltpu.make_async_copy(q_hbm.at[pl.ds(4 * half, 4)], qall.at[chunk(half, 0, 0)], qsem.at[half])
        copy.start()
        own_copies.append(copy)
    c_tk, c_tv = local_copy(1, tk_hbm, tkb), local_copy(2, tv_hbm, tvb)
    c_nk, c_nv = local_copy(3, nk_hbm, nkb), local_copy(4, nv_hbm, nvb)
    c_w = local_copy(7, w_hbm, wb)

    def gathered(half, dp, dq):
        received(qall.at[chunk(half, dp, dq)], gs.at[half, 0], gr.at[half, dp, dq])

    def forward(dp):
        for half in (0, 1):
            gathered(half, dp, 0)
            for k in (2, 1, 3):
                ref = qall.at[chunk(half, dp, 0)]
                send(ref, ref, gs.at[half, 3 + dp * 3 + k - 1], gr.at[half, dp, (4 - k) % 4], along(half, 1, k))

    c_sr.wait()
    c_tl.wait()
    lane8 = iota((8, 128), 1)
    at_slot = jnp.full((8, 128), -1, I32)
    slot_of = jnp.zeros((8, 128), I32)
    for j in range(SLOTS):
        request = sr[j]
        home, half, fourth = request // 8, (request % 8) // 4, request % 4
        swapped = (home % 4) * 4 + home // 4
        position = half * 64 + jnp.where(half == 0, home, swapped) * 4 + fourth
        at_slot = jnp.where(lane8 == j, position, at_slot)
        slot_of = jnp.where(lane8 == position, j, slot_of)
    ivec[...] = slot_of
    c_inv = pltpu.make_async_copy(ivec, inv, lsem.at[8])
    c_inv.start()
    here = (jnp.broadcast_to(at_slot[0:1], (REQ, 128)) == iota((REQ, 128), 0)).astype(F32)
    absent[...] = jnp.broadcast_to((1.0 - jnp.sum(here, axis=1, keepdims=True)) * VERY_LOW, (REQ, 128))
    l1[...] = jnp.zeros_like(l1)
    lloc[...] = jnp.zeros_like(lloc)

    def home_part():
        c_qown.wait()
        c_tk.wait()
        c_tv.wait()
        c_nk.wait()
        c_nv.wait()
        new_scores = lax.dot_general(qown[...].reshape(OWN * R, HD), nkb[...], NT, preferred_element_type=F32)
        token = iota((R, 256), 1)
        new_lane, step = iota((R, 32), 1), iota((R, 32), 0) // 8
        lane, log_columns = iota((R, 128), 1), jnp.zeros((R, 128), F32)
        for r in range(OWN):
            old = lax.dot_general(qown[r], tkb[r], NT, preferred_element_type=F32)
            old = jnp.where(token < tl[r], old, VERY_LOW)
            new = new_scores[r * R : (r + 1) * R]
            new = jnp.where((new_lane >= 4 * r) & (new_lane <= 4 * r + step), new, VERY_LOW)
            peak = jnp.maximum(jnp.max(old, axis=1, keepdims=True), jnp.max(new, axis=1, keepdims=True))
            old = jnp.exp2((old - peak) * SCALE2)
            new = jnp.exp2((new - peak) * SCALE2)
            total = jnp.sum(old, axis=1, keepdims=True) + jnp.sum(new, axis=1, keepdims=True)
            result = jnp.dot(old.astype(BF16), tvb[r], preferred_element_type=F32)
            result = result + jnp.dot(new.astype(BF16), nvb[...], preferred_element_type=F32)
            lo[r] = (result * (1.0 / total)).astype(BF16)
            log_columns = jnp.where(lane == r, peak * SCALE2 + jnp.log2(total), log_columns)
        pick = (iota((OWN, 128), 0) == iota((OWN, 128), 1)).astype(F32).astype(BF16)
        rows = to_rows(pick, log_columns)
        lloc[0, 0:4] = rows[0:4]
        lloc[1, 0:4] = rows[4:8]

    def lend(dp):
        lane, zeros = iota((R, 128), 1), jnp.zeros((R, HD), BF16)
        bases = []
        for half in (0, 1):
            p, _ = place(half)
            bases.append(pl.multiple_of(half * 64 + ((p + dp) % 4) * 16, 16))
        log_columns = [jnp.zeros((R, 128), F32)] * 2
        todo = [(half, i) for half in (0, 1) for i in range(0, 16, 2)]
        for first in range(0, len(todo), PAIRS):
            batch = todo[first : first + PAIRS]
            slots = [[inv[0, bases[half] + i + u] for u in (0, 1)] for half, i in batch]
            scores = []
            for (half, i), (a, b) in zip(batch, slots):
                queries = [qall[bases[half] + i + u] for u in (0, 1)]
                queries = [jnp.concatenate([queries[0], zeros], axis=1), jnp.concatenate([zeros, queries[1]], axis=1)]
                keys = jnp.concatenate([kb[a], kb[b]], axis=1)
                scores.append(lax.dot_general(jnp.concatenate(queries, axis=0), keys, NT, preferred_element_type=F32))
            peaks = [jnp.max(score, axis=1, keepdims=True) for score in scores]
            terms = [jnp.exp2((score - peak) * SCALE2) for score, peak in zip(scores, peaks)]
            totals = [jnp.sum(term, axis=1, keepdims=True) for term in terms]
            for (half, i), (a, b), peak, term, total in zip(batch, slots, peaks, terms, totals):
                values = jnp.concatenate([vb[a], vb[b]], axis=1)
                result = jnp.dot(term.astype(BF16), values, preferred_element_type=F32)
                inverse = 1.0 / total
                logs = peak * SCALE2 + jnp.log2(total)
                omsg[bases[half] + i] = (result[:R, :HD] * inverse[:R]).astype(BF16)
                omsg[bases[half] + i + 1] = (result[R:, HD:] * inverse[R:]).astype(BF16)
                log_columns[half] = jnp.where(lane == i, logs[:R], log_columns[half])
                log_columns[half] = jnp.where(lane == i + 1, logs[R:], log_columns[half])
        pick = (iota((16, 128), 0) == iota((16, 128), 1)).astype(F32).astype(BF16)
        for half in (0, 1):
            part = pl.ds(bases[half], 16)
            lmsg[part] = to_rows(pick, log_columns[half]) + absent[part]
            if dp:
                to = along(half, 0, dp)
                send(omsg.at[part], ro1.at[half, dp - 1], s1.at[half, dp - 1, 1], r1.at[half, dp - 1, 1], to)
                send(lmsg.at[part], rl1.at[half, dp - 1], s1.at[half, dp - 1, 0], r1.at[half, dp - 1, 0], to)

    def first_merge(half):
        p, q = place(half)
        base = pl.multiple_of(half * 64 + p * 16, 16)
        for k in FIRST:
            received(rl1.at[half, k - 1], s1.at[half, 0, 0], r1.at[half, k - 1, 0])
            received(ro1.at[half, k - 1], s1.at[half, 0, 0], r1.at[half, k - 1, 1])
        weights, log = merge_weights([lmsg[pl.ds(base, 16)]] + [rl1[half, k] for k in range(3)])
        weights = by_lane_group(weights)
        for i in range(4):
            l1[half, i, 0:4] = log[4 * i : 4 * i + 4]
        for i in range(0, 16, 4):
            parts = [[omsg[base + i + u]] + [ro1[half, k, i + u] for k in range(3)] for u in range(4)]
            for u, result in enumerate(scaled_sums(weights[i : i + 4], parts)):
                m1[half, i + u] = result.astype(BF16)
        for k in (2, 1, 3):
            other = (q + k) % 4
            to = along(half, 1, k)
            send(m1.at[half, pl.ds(other * 4, 4)], ro2.at[half, k - 1], s2.at[half, k - 1, 1], r2.at[half, k - 1, 1], to)
            send(l1.at[half, other], rl2.at[half, k - 1], s2.at[half, k - 1, 0], r2.at[half, k - 1, 0], to)

    def second_merge(half):
        _, q = place(half)
        for k in (1, 3, 2):
            received(rl2.at[half, k - 1], s2.at[half, 0, 0], r2.at[half, k - 1, 0])
            received(ro2.at[half, k - 1], s2.at[half, 0, 0], r2.at[half, k - 1, 1])
        weights, _ = merge_weights([l1[half, q]] + [rl2[half, k] for k in range(3)] + [lloc[half]])
        lent, home = by_lane_group(weights[:4]), weights[4]
        parts = [[m1[half, q * 4 + u]] + [ro2[half, k, u] for k in range(3)] for u in range(4)]
        lane, row = iota((R, 128), 1), iota((R, 128), 0)
        picked = [
            jnp.where(lane == row + u * R, jnp.broadcast_to(home[u : u + 1], (R, 128)), 0.0).astype(BF16) for u in range(4)
        ]
        homes = jnp.concatenate([lo[half * 4 + u] for u in range(4)], axis=0)
        own = jnp.dot(jnp.concatenate(picked, axis=0), homes, preferred_element_type=F32)
        for u, result in enumerate(scaled_sums(lent[0:4], parts)):
            att[(half * 4 + u) * R : (half * 4 + u + 1) * R] = result + own[u * R : (u + 1) * R]

    order = (0,) + FORWARD
    home_part()
    for dp in FORWARD:
        forward(dp)
    c_inv.wait()
    for copy in own_copies:
        copy.wait()
    for dp in order:
        for half in (0, 1):
            for dq in (1, 3, 2):
                gathered(half, dp, dq)
        if dp == 0:
            c_k.wait()
            c_v.wait()
        lend(dp)
    for half in (0, 1):
        first_merge(half)
    for half in (0, 1):
        second_merge(half)

    flat = jnp.concatenate([att[pl.ds(h, R, stride=8)].astype(BF16) for h in range(8)], axis=1)
    c_w.wait()

    def columns(target):
        return jnp.dot(flat, wb[:, pl.ds(pl.multiple_of(target * 1024, 1024), 1024)], preferred_element_type=F32)

    for dy in (2, 1, 3, 0):
        cs[dy] = columns(((y + dy) % 4) * 2 + 1 - c).astype(BF16)
        send(cs.at[dy], cr.at[dy], css.at[dy], crs.at[dy], {"tp": y * 2 + 1 - c})
    value = None
    for dy in (2, 1, 3, 0):
        value = columns(((y + dy) % 4) * 2 + c)
        received(cr.at[dy], css.at[dy], crs.at[dy])
        value = value + cr[dy].astype(F32)
        if dy:
            ys[dy - 1] = value.astype(BF16)
            send(ys.at[dy - 1], yr.at[dy - 1], yss.at[dy - 1], yrs.at[dy - 1], {"tp": ((y + dy) % 4) * 2 + c})
    for dy in (2, 1, 3):
        received(yr.at[dy - 1], yss.at[dy - 1], yrs.at[dy - 1])
        value = value + yr[dy - 1].astype(F32)
    out[...] = value.astype(BF16)
    for copy in sent:
        copy.wait_send()


def per_device(
    queries, tail_keys, tail_values, new_keys, new_values, tail_lengths, pool_keys, pool_values, slot_request, out_weight
):
    in_hbm = pl.BlockSpec(memory_space=pltpu.HBM)
    dma = pltpu.SemaphoreType.DMA

    def v(*shape, dtype=BF16):
        return pltpu.VMEM(shape, dtype)

    args = (
        slot_request,
        tail_lengths,
        queries.reshape(OWN, R, HD),
        tail_keys.reshape(OWN, 256, HD),
        tail_values.reshape(OWN, 256, HD),
        new_keys.reshape(R, HD),
        new_values.reshape(R, HD),
        pool_keys.reshape(SLOTS, 256, HD),
        pool_values.reshape(SLOTS, 256, HD),
        out_weight,
    )
    result = pl.pallas_call(
        kernel,
        out_shape=jax.ShapeDtypeStruct((R, 1024), BF16),
        in_specs=[in_hbm] * len(args),
        out_specs=pl.BlockSpec(memory_space=pltpu.VMEM),
        scratch_shapes=[
            v(REQ, R, HD), v(OWN, R, HD), v(SLOTS, 256, HD), v(SLOTS, 256, HD), v(OWN, 256, HD), v(OWN, 256, HD),
            v(R, HD), v(R, HD), v(1024, 8192),
            v(REQ, R, HD), v(REQ, 128, dtype=F32), v(REQ, 128, dtype=F32),
            v(2, 3, 16, R, HD), v(2, 3, 16, 128, dtype=F32),
            v(2, 16, R, HD), v(2, 4, 8, 128, dtype=F32),
            v(2, 3, 4, R, HD), v(2, 3, 8, 128, dtype=F32),
            v(OWN, R, HD), v(2, 8, 128, dtype=F32), v(OWN * R, HD, dtype=F32),
            v(4, R, 1024), v(4, R, 1024), v(3, R, 1024), v(3, R, 1024),
            pltpu.SMEM((SLOTS,), I32), pltpu.SMEM((OWN,), I32), v(8, 128, dtype=I32), pltpu.SMEM((8, 128), I32),
            dma((11,)), dma((2,)), dma((2, 15)), dma((2, 4, 4)),
            dma((2, 3, 2)), dma((2, 3, 2)), dma((2, 3, 2)), dma((2, 3, 2)),
            dma((4,)), dma((4,)), dma((3,)), dma((3,)),
        ],
        name="lent_attention",
        compiler_params=pltpu.CompilerParams(collective_id=0, has_side_effects=True, vmem_limit_bytes=44 * 2**20),
    )(*[pltpu.with_memory_space_constraint(arg, pltpu.HBM) for arg in args])
    return result.reshape(OWN, 4, 1024)


def solution(mesh):
    placed = (
        P("inst", None, "tp", None),
        P("inst", "tp", None, None),
        P("inst", "tp", None, None),
        P("inst", None, "tp", None),
        P("inst", None, "tp", None),
        P("inst"),
        P("inst", "tp", None, None),
        P("inst", "tp", None, None),
        P("inst"),
        P("tp", None),
    )
    return jax.shard_map(
        per_device, mesh=mesh, in_specs=placed, out_specs=P("inst", None, "tp"), check_vma=False
    )
```

time: 48 us -> 39 us (0.81)
  local copies, waits for them, and re-layouts: 6.28 us -> 0.66 us
  Pallas kernels: 41.3 us -> 38.2 us
    unnamed x14 -> x0, local copies, waits for them, and re-layouts: 5.62 us -> none
    pallas_call x1, Pallas kernels: 41.3 us -> 38.2 us  [per_device(): pl.pallas_call(kernel, out_shape=jax.ShapeDtypeStruct((R, 1024), BF16), i...]
    another operation x1 -> x0, local copies, waits for them, and re-layouts: 0.66 us -> none  [per_device(): return result.transpose(1, 0, 2, 3).reshape(OWN, 4, 1024)]
    reshape x0 -> x1, local copies, waits for them, and re-layouts: none -> 0.66 us  [per_device(): return result.reshape(OWN, 4, 1024)]
where the time goes in v2:
time: 39 us; the launch traced here: 38.9 us
  Pallas kernels  38.2 us (98%)
  local copies, waits for them, and re-layouts  0.66 us (2%)
    pallas_call x1, Pallas kernels, per_device(): pl.pallas_call(kernel, out_shape=jax.ShapeDtypeStruct((R, 1024), BF16), i...  38.2 us

profile of v2, /device:TPU:1, one launch (start us, length us, event | category | flops | bytes accessed | tf_op | source)
XLA Modules:
  0.0 38.9 jit_solution(4156703124283929905)
XLA Ops:
  0.0 38.2 %lent_attention.1 = bf16[32,1024]{1,0:T(8,128)(2,1)S(1)} custom-call(s32[48]{0:T(128)} %sr_hbm.1, s32[8]{0:T(128)} %tl_hbm.1, bf16[8,32,128]{2,1,0:T(8,128)(2,1)} %bitcast.11, bf16[8,256,128]{2,1,0:T(8,128)(2,1)} %bitcast.9, bf16[8,256,128]{2,1,0:T(8,128)(2,1)} %bitcast.10, bf16[32,128]{1,0:T(8,128)(2,1)} %bitcast.12, bf16[32,128]{1,0:T(8,128)(2,1)} %bitcast.13, ...), custom_call_target="tpu_custom_call" | custom-call | tf_op jit(solution)/shard_map/lent_attention/pallas_call | solution.py:343
  38.3 0.7 %reshape.31 = bf16[8,4,1024]{2,1,0:T(4,128)(2,1)} reshape(bf16[32,1024]{1,0:T(8,128)(2,1)S(1)} %lent_attention.1) | data formatting | bytes 131072 | tf_op jit(solution)/shard_map/reshape | solution.py:365

commit v3 on v2

--- a/solution.py
+++ b/solution.py
@@ -19,7 +19,14 @@
 OWN = 8
 REQ = 128
 R = 32
-PAIRS = 16
+GROUPS = (
+    ((0, 0), (0, 1), (0, 3), (0, 2)),
+    ((2, 0), (3, 0), (1, 0)),
+    ((2, 1), (2, 3), (2, 2)),
+    ((3, 1), (3, 3), (3, 2)),
+    ((1, 1), (1, 3), (1, 2)),
+)
+GATHER = 30
 FORWARD = (2, 3, 1)
 FIRST = (2, 1, 3)
 
@@ -113,6 +120,11 @@
         copy = remote(src, dst, ss, rs, device)
         copy.start()
         sent.append(copy)
+
+    def all_sent():
+        for copy in sent:
+            copy.wait_send()
+        del sent[:]
 
     def received(dst, ss, rs):
         remote(dst, dst, ss, rs, along(0, 0, 1)).wait_recv()
@@ -199,54 +211,64 @@
         lloc[0, 0:4] = rows[0:4]
         lloc[1, 0:4] = rows[4:8]
 
-    def lend(dp):
+    def lend(chunks):
         lane, zeros = iota((R, 128), 1), jnp.zeros((R, HD), BF16)
-        bases = []
+        todo = []
+        for half, dp, dq in chunks:
+            p, q = place(half)
+            line, column = (p + dp) % 4, ((q + dq) % 4) * 4
+            base = pl.multiple_of(half * 64 + line * 16 + column, 4)
+            todo += [((half, dp), base + i, column + i) for i in (0, 2)]
+        log_columns = {}
+        for half, dp, _ in chunks:
+            if (half, dp) not in log_columns:
+                log_columns[half, dp] = logs_of[half, dp]
+        slots = [[inv[0, first + u] for u in (0, 1)] for _, first, _ in todo]
+        scores = []
+        for (_, first, _), (a, b) in zip(todo, slots):
+            queries = [qall[first + u] for u in (0, 1)]
+            queries = [jnp.concatenate([queries[0], zeros], axis=1), jnp.concatenate([zeros, queries[1]], axis=1)]
+            keys = jnp.concatenate([kb[a], kb[b]], axis=1)
+            scores.append(lax.dot_general(jnp.concatenate(queries, axis=0), keys, NT, preferred_element_type=F32))
+        peaks = [jnp.max(score, axis=1, keepdims=True) for score in scores]
+        terms = [jnp.exp2((score - peak) * SCALE2) for score, peak in zip(scores, peaks)]
+        totals = [jnp.sum(term, axis=1, keepdims=True) for term in terms]
+        for (key, first, column), (a, b), peak, term, total in zip(todo, slots, peaks, terms, totals):
+            values = jnp.concatenate([vb[a], vb[b]], axis=1)
+            result = jnp.dot(term.astype(BF16), values, preferred_element_type=F32)
+            inverse = 1.0 / total
+            logs = peak * SCALE2 + jnp.log2(total)
+            omsg[first] = (result[:R, :HD] * inverse[:R]).astype(BF16)
+            omsg[first + 1] = (result[R:, HD:] * inverse[R:]).astype(BF16)
+            log_columns[key] = jnp.where(lane == column, logs[:R], log_columns[key])
+            log_columns[key] = jnp.where(lane == column + 1, logs[R:], log_columns[key])
+        for key in log_columns:
+            logs_of[key] = log_columns[key]
+
+    def send_line(dp):
+        pick = (iota((16, 128), 0) == iota((16, 128), 1)).astype(F32).astype(BF16)
+        parts = []
         for half in (0, 1):
             p, _ = place(half)
-            bases.append(pl.multiple_of(half * 64 + ((p + dp) % 4) * 16, 16))
-        log_columns = [jnp.zeros((R, 128), F32)] * 2
-        todo = [(half, i) for half in (0, 1) for i in range(0, 16, 2)]
-        for first in range(0, len(todo), PAIRS):
-            batch = todo[first : first + PAIRS]
-            slots = [[inv[0, bases[half] + i + u] for u in (0, 1)] for half, i in batch]
-            scores = []
-            for (half, i), (a, b) in zip(batch, slots):
-                queries = [qall[bases[half] + i + u] for u in (0, 1)]
-                queries = [jnp.concatenate([queries[0], zeros], axis=1), jnp.concatenate([zeros, queries[1]], axis=1)]
-                keys = jnp.concatenate([kb[a], kb[b]], axis=1)
-                scores.append(lax.dot_general(jnp.concatenate(queries, axis=0), keys, NT, preferred_element_type=F32))
-            peaks = [jnp.max(score, axis=1, keepdims=True) for score in scores]
-            terms = [jnp.exp2((score - peak) * SCALE2) for score, peak in zip(scores, peaks)]
-            totals = [jnp.sum(term, axis=1, keepdims=True) for term in terms]
-            for (half, i), (a, b), peak, term, total in zip(batch, slots, peaks, terms, totals):
-                values = jnp.concatenate([vb[a], vb[b]], axis=1)
-                result = jnp.dot(term.astype(BF16), values, preferred_element_type=F32)
-                inverse = 1.0 / total
-                logs = peak * SCALE2 + jnp.log2(total)
-                omsg[bases[half] + i] = (result[:R, :HD] * inverse[:R]).astype(BF16)
-                omsg[bases[half] + i + 1] = (result[R:, HD:] * inverse[R:]).astype(BF16)
-                log_columns[half] = jnp.where(lane == i, logs[:R], log_columns[half])
-                log_columns[half] = jnp.where(lane == i + 1, logs[R:], log_columns[half])
-        pick = (iota((16, 128), 0) == iota((16, 128), 1)).astype(F32).astype(BF16)
-        for half in (0, 1):
-            part = pl.ds(bases[half], 16)
-            lmsg[part] = to_rows(pick, log_columns[half]) + absent[part]
+            parts.append(pl.ds(pl.multiple_of(half * 64 + ((p + dp) % 4) * 16, 16), 16))
             if dp:
-                to = along(half, 0, dp)
-                send(omsg.at[part], ro1.at[half, dp - 1], s1.at[half, dp - 1, 1], r1.at[half, dp - 1, 1], to)
-                send(lmsg.at[part], rl1.at[half, dp - 1], s1.at[half, dp - 1, 0], r1.at[half, dp - 1, 0], to)
+                send(omsg.at[parts[half]], ro1.at[half, dp - 1], s1.at[half, dp - 1, 0], r1.at[half, dp - 1, 0], along(half, 0, dp))
+        for half, part in enumerate(parts):
+            lmsg[part] = to_rows(pick, logs_of[half, dp]) + absent[part]
+            if dp:
+                send(lmsg.at[part], rl1.at[half, dp - 1], s1.at[half, dp - 1, 1], r1.at[half, dp - 1, 1], along(half, 0, dp))
 
     def first_merge(half):
         p, q = place(half)
         base = pl.multiple_of(half * 64 + p * 16, 16)
         for k in FIRST:
-            received(rl1.at[half, k - 1], s1.at[half, 0, 0], r1.at[half, k - 1, 0])
-            received(ro1.at[half, k - 1], s1.at[half, 0, 0], r1.at[half, k - 1, 1])
+            received(rl1.at[half, k - 1], s1.at[half, 0, 0], r1.at[half, k - 1, 1])
         weights, log = merge_weights([lmsg[pl.ds(base, 16)]] + [rl1[half, k] for k in range(3)])
         weights = by_lane_group(weights)
         for i in range(4):
             l1[half, i, 0:4] = log[4 * i : 4 * i + 4]
+        for k in FIRST:
+            received(ro1.at[half, k - 1], s1.at[half, 0, 0], r1.at[half, k - 1, 0])
         for i in range(0, 16, 4):
             parts = [[omsg[base + i + u]] + [ro1[half, k, i + u] for k in range(3)] for u in range(4)]
             for u, result in enumerate(scaled_sums(weights[i : i + 4], parts)):
@@ -261,36 +283,47 @@
         _, q = place(half)
         for k in (1, 3, 2):
             received(rl2.at[half, k - 1], s2.at[half, 0, 0], r2.at[half, k - 1, 0])
-            received(ro2.at[half, k - 1], s2.at[half, 0, 0], r2.at[half, k - 1, 1])
         weights, _ = merge_weights([l1[half, q]] + [rl2[half, k] for k in range(3)] + [lloc[half]])
         lent, home = by_lane_group(weights[:4]), weights[4]
-        parts = [[m1[half, q * 4 + u]] + [ro2[half, k, u] for k in range(3)] for u in range(4)]
         lane, row = iota((R, 128), 1), iota((R, 128), 0)
         picked = [
             jnp.where(lane == row + u * R, jnp.broadcast_to(home[u : u + 1], (R, 128)), 0.0).astype(BF16) for u in range(4)
         ]
         homes = jnp.concatenate([lo[half * 4 + u] for u in range(4)], axis=0)
         own = jnp.dot(jnp.concatenate(picked, axis=0), homes, preferred_element_type=F32)
+        for k in (1, 3, 2):
+            received(ro2.at[half, k - 1], s2.at[half, 0, 0], r2.at[half, k - 1, 1])
+        parts = [[m1[half, q * 4 + u]] + [ro2[half, k, u] for k in range(3)] for u in range(4)]
         for u, result in enumerate(scaled_sums(lent[0:4], parts)):
             att[(half * 4 + u) * R : (half * 4 + u + 1) * R] = result + own[u * R : (u + 1) * R]
 
-    order = (0,) + FORWARD
     home_part()
     for dp in FORWARD:
         forward(dp)
     c_inv.wait()
     for copy in own_copies:
         copy.wait()
-    for dp in order:
-        for half in (0, 1):
-            for dq in (1, 3, 2):
+    logs_of = {(half, dp): jnp.zeros((R, 128), F32) for half in (0, 1) for dp in range(4)}
+    c_k.wait()
+    c_v.wait()
+    seen = {0: 0, 1: 0, 2: 0, 3: 0}
+    for pairs in GROUPS:
+        chunks = [(half, dp, dq) for dp, dq in pairs for half in (0, 1)]
+        for half, dp, dq in chunks:
+            if dq:
                 gathered(half, dp, dq)
-        if dp == 0:
-            c_k.wait()
-            c_v.wait()
-        lend(dp)
+        lend(chunks)
+        for dp, dq in pairs:
+            seen[dp] += 1
+        for dp in sorted({dp for dp, _ in pairs if seen[dp] == 4}):
+            send_line(dp)
+    lent = sent[GATHER:]
+    del sent[GATHER:]
+    all_sent()
     for half in (0, 1):
         first_merge(half)
+    for copy in lent:
+        copy.wait_send()
     for half in (0, 1):
         second_merge(half)
 
@@ -300,22 +333,35 @@
     def columns(target):
         return jnp.dot(flat, wb[:, pl.ds(pl.multiple_of(target * 1024, 1024), 1024)], preferred_element_type=F32)
 
-    for dy in (2, 1, 3, 0):
+    def share(dy):
         cs[dy] = columns(((y + dy) % 4) * 2 + 1 - c).astype(BF16)
         send(cs.at[dy], cr.at[dy], css.at[dy], crs.at[dy], {"tp": y * 2 + 1 - c})
-    value = None
-    for dy in (2, 1, 3, 0):
+
+    def both(dy):
         value = columns(((y + dy) % 4) * 2 + c)
         received(cr.at[dy], css.at[dy], crs.at[dy])
-        value = value + cr[dy].astype(F32)
-        if dy:
-            ys[dy - 1] = value.astype(BF16)
-            send(ys.at[dy - 1], yr.at[dy - 1], yss.at[dy - 1], yrs.at[dy - 1], {"tp": ((y + dy) % 4) * 2 + c})
+        return value + cr[dy].astype(F32)
+
+    def along_y(dy):
+        ys[dy - 1] = both(dy).astype(BF16)
+        send(ys.at[dy - 1], yr.at[dy - 1], yss.at[dy - 1], yrs.at[dy - 1], {"tp": ((y + dy) % 4) * 2 + c})
+
+    share(2)
+    share(1)
+    share(3)
+    along_y(2)
+    along_y(1)
+    along_y(3)
+    share(0)
+    value = both(0)
+    last = sent[-4:]
+    del sent[-4:]
+    all_sent()
     for dy in (2, 1, 3):
         received(yr.at[dy - 1], yss.at[dy - 1], yrs.at[dy - 1])
         value = value + yr[dy - 1].astype(F32)
     out[...] = value.astype(BF16)
-    for copy in sent:
+    for copy in last:
         copy.wait_send()
 
 

time: 39 us -> 38.8 us (level)
  no operation moved by 1% of the time
where the time goes in v3:
time: 38.8 us; the launch traced here: 38.7 us
  Pallas kernels  38.1 us (98%)
  local copies, waits for them, and re-layouts  0.66 us (2%)
    pallas_call x1, Pallas kernels, per_device(): pl.pallas_call(kernel, out_shape=jax.ShapeDtypeStruct((R, 1024), BF16), i...  38.1 us

profile of v3, /device:TPU:1, one launch (start us, length us, event | category | flops | bytes accessed | tf_op | source)
XLA Modules:
  0.0 38.7 jit_solution(6472655248312528972)
XLA Ops:
  0.0 38.1 %lent_attention.1 = bf16[32,1024]{1,0:T(8,128)(2,1)S(1)} custom-call(s32[48]{0:T(128)} %sr_hbm.1, s32[8]{0:T(128)} %tl_hbm.1, bf16[8,32,128]{2,1,0:T(8,128)(2,1)} %bitcast.11, bf16[8,256,128]{2,1,0:T(8,128)(2,1)} %bitcast.9, bf16[8,256,128]{2,1,0:T(8,128)(2,1)} %bitcast.10, bf16[32,128]{1,0:T(8,128)(2,1)} %bitcast.12, bf16[32,128]{1,0:T(8,128)(2,1)} %bitcast.13, ...), custom_call_target="tpu_custom_call" | custom-call | tf_op jit(solution)/shard_map/lent_attention/pallas_call | solution.py:389
  38.1 0.7 %reshape.31 = bf16[8,4,1024]{2,1,0:T(4,128)(2,1)} reshape(bf16[32,1024]{1,0:T(8,128)(2,1)S(1)} %lent_attention.1) | data formatting | bytes 131072 | tf_op jit(solution)/shard_map/reshape | solution.py:411

commit v4 on v3

--- a/solution.py
+++ b/solution.py
@@ -26,6 +26,7 @@
     ((3, 1), (3, 3), (3, 2)),
     ((1, 1), (1, 3), (1, 2)),
 )
+EARLY = 4
 GATHER = 30
 FORWARD = (2, 3, 1)
 FIRST = (2, 1, 3)
@@ -95,9 +96,6 @@
             return {"inst": ((z + k) % 4) * 4 + x}
         return {"inst": z * 4 + (x + k) % 4}
 
-    def place(half):
-        return (z, x) if half == 0 else (x, z)
-
     barrier = pltpu.get_barrier_semaphore()
     peers = [along(0, axis, k) for axis in (0, 1) for k in (2, 1, 3)]
     peers += [{"tp": ((y + k) % 4) * 2 + c} for k in (2, 1, 3)] + [{"tp": y * 2 + 1 - c}]
@@ -130,23 +128,23 @@
         remote(dst, dst, ss, rs, along(0, 0, 1)).wait_recv()
 
     def chunk(half, dp, dq):
-        p, q = place(half)
-        return pl.ds(half * 64 + (((p + dp) % 4) * 4 + (q + dq) % 4) * 4, 4)
-
+        return pl.ds(half * 64 + dp * 16 + dq * 4, 4)
+
+    c_qown.wait()
     for axis in (0, 1):
         for k in (2, 1, 3):
             for half in (0, 1):
                 back = (4 - k) % 4
                 send(
-                    q_hbm.at[pl.ds(4 * half, 4)],
-                    qall.at[chunk(half, 0, 0)],
+                    qown.at[pl.ds(4 * half, 4)],
+                    qall.at[chunk(half, back, 0) if axis == 0 else chunk(half, 0, back)],
                     gs.at[half, axis * 3 + k - 1],
                     gr.at[half, back, 0] if axis == 0 else gr.at[half, 0, back],
                     along(half, axis, k),
                 )
     own_copies = []
     for half in (0, 1):
-        copy = pltpu.make_async_copy(q_hbm.at[pl.ds(4 * half, 4)], qall.at[chunk(half, 0, 0)], qsem.at[half])
+        copy = pltpu.make_async_copy(qown.at[pl.ds(4 * half, 4)], qall.at[chunk(half, 0, 0)], qsem.at[half])
         copy.start()
         own_copies.append(copy)
     c_tk, c_tv = local_copy(1, tk_hbm, tkb), local_copy(2, tv_hbm, tvb)
@@ -160,8 +158,8 @@
         for half in (0, 1):
             gathered(half, dp, 0)
             for k in (2, 1, 3):
-                ref = qall.at[chunk(half, dp, 0)]
-                send(ref, ref, gs.at[half, 3 + dp * 3 + k - 1], gr.at[half, dp, (4 - k) % 4], along(half, 1, k))
+                to = qall.at[chunk(half, dp, (4 - k) % 4)]
+                send(qall.at[chunk(half, dp, 0)], to, gs.at[half, 3 + dp * 3 + k - 1], gr.at[half, dp, (4 - k) % 4], along(half, 1, k))
 
     c_sr.wait()
     c_tl.wait()
@@ -171,8 +169,8 @@
     for j in range(SLOTS):
         request = sr[j]
         home, half, fourth = request // 8, (request % 8) // 4, request % 4
-        swapped = (home % 4) * 4 + home // 4
-        position = half * 64 + jnp.where(half == 0, home, swapped) * 4 + fourth
+        dz, dx = (home // 4 - z + 4) % 4, (home % 4 - x + 4) % 4
+        position = half * 64 + jnp.where(half == 0, dz * 4 + dx, dx * 4 + dz) * 4 + fourth
         at_slot = jnp.where(lane8 == j, position, at_slot)
         slot_of = jnp.where(lane8 == position, j, slot_of)
     ivec[...] = slot_of
@@ -184,7 +182,6 @@
     lloc[...] = jnp.zeros_like(lloc)
 
     def home_part():
-        c_qown.wait()
         c_tk.wait()
         c_tv.wait()
         c_nk.wait()
@@ -215,10 +212,7 @@
         lane, zeros = iota((R, 128), 1), jnp.zeros((R, HD), BF16)
         todo = []
         for half, dp, dq in chunks:
-            p, q = place(half)
-            line, column = (p + dp) % 4, ((q + dq) % 4) * 4
-            base = pl.multiple_of(half * 64 + line * 16 + column, 4)
-            todo += [((half, dp), base + i, column + i) for i in (0, 2)]
+            todo += [((half, dp), half * 64 + dp * 16 + dq * 4 + i, dq * 4 + i) for i in (0, 2)]
         log_columns = {}
         for half, dp, _ in chunks:
             if (half, dp) not in log_columns:
@@ -247,43 +241,52 @@
 
     def send_line(dp):
         pick = (iota((16, 128), 0) == iota((16, 128), 1)).astype(F32).astype(BF16)
-        parts = []
         for half in (0, 1):
-            p, _ = place(half)
-            parts.append(pl.ds(pl.multiple_of(half * 64 + ((p + dp) % 4) * 16, 16), 16))
-            if dp:
-                send(omsg.at[parts[half]], ro1.at[half, dp - 1], s1.at[half, dp - 1, 0], r1.at[half, dp - 1, 0], along(half, 0, dp))
-        for half, part in enumerate(parts):
+            send_part(half, dp, EARLY if dp in (1, 3) else 0, 16)
+        for half in (0, 1):
+            part = pl.ds(half * 64 + dp * 16, 16)
             lmsg[part] = to_rows(pick, logs_of[half, dp]) + absent[part]
             if dp:
-                send(lmsg.at[part], rl1.at[half, dp - 1], s1.at[half, dp - 1, 1], r1.at[half, dp - 1, 1], along(half, 0, dp))
+                send(lmsg.at[part], rl1.at[half, dp - 1], s1.at[half, dp - 1, 2], r1.at[half, dp - 1, 2], along(half, 0, dp))
+        if dp == 2 and EARLY:
+            for half in (0, 1):
+                for other in (3, 1):
+                    send_part(half, other, 0, EARLY)
+
+    def send_part(half, dp, start, end):
+        if dp:
+            send(
+                omsg.at[pl.ds(half * 64 + dp * 16 + start, end - start)],
+                ro1.at[half, dp - 1, pl.ds(start, end - start)],
+                s1.at[half, dp - 1, int(start > 0)],
+                r1.at[half, dp - 1, int(start > 0)],
+                along(half, 0, dp),
+            )
 
     def first_merge(half):
-        p, q = place(half)
-        base = pl.multiple_of(half * 64 + p * 16, 16)
+        base = half * 64
         for k in FIRST:
-            received(rl1.at[half, k - 1], s1.at[half, 0, 0], r1.at[half, k - 1, 1])
+            received(rl1.at[half, k - 1], s1.at[half, 0, 0], r1.at[half, k - 1, 2])
         weights, log = merge_weights([lmsg[pl.ds(base, 16)]] + [rl1[half, k] for k in range(3)])
         weights = by_lane_group(weights)
         for i in range(4):
             l1[half, i, 0:4] = log[4 * i : 4 * i + 4]
         for k in FIRST:
-            received(ro1.at[half, k - 1], s1.at[half, 0, 0], r1.at[half, k - 1, 0])
+            for start, end in ((0, EARLY), (EARLY, 16)) if EARLY and k != 2 else ((0, 16),):
+                received(ro1.at[half, k - 1, pl.ds(start, end - start)], s1.at[half, 0, 0], r1.at[half, k - 1, int(start > 0)])
         for i in range(0, 16, 4):
             parts = [[omsg[base + i + u]] + [ro1[half, k, i + u] for k in range(3)] for u in range(4)]
             for u, result in enumerate(scaled_sums(weights[i : i + 4], parts)):
                 m1[half, i + u] = result.astype(BF16)
         for k in (2, 1, 3):
-            other = (q + k) % 4
             to = along(half, 1, k)
-            send(m1.at[half, pl.ds(other * 4, 4)], ro2.at[half, k - 1], s2.at[half, k - 1, 1], r2.at[half, k - 1, 1], to)
-            send(l1.at[half, other], rl2.at[half, k - 1], s2.at[half, k - 1, 0], r2.at[half, k - 1, 0], to)
+            send(m1.at[half, pl.ds(k * 4, 4)], ro2.at[half, k - 1], s2.at[half, k - 1, 1], r2.at[half, k - 1, 1], to)
+            send(l1.at[half, k], rl2.at[half, k - 1], s2.at[half, k - 1, 0], r2.at[half, k - 1, 0], to)
 
     def second_merge(half):
-        _, q = place(half)
         for k in (1, 3, 2):
             received(rl2.at[half, k - 1], s2.at[half, 0, 0], r2.at[half, k - 1, 0])
-        weights, _ = merge_weights([l1[half, q]] + [rl2[half, k] for k in range(3)] + [lloc[half]])
+        weights, _ = merge_weights([l1[half, 0]] + [rl2[half, k] for k in range(3)] + [lloc[half]])
         lent, home = by_lane_group(weights[:4]), weights[4]
         lane, row = iota((R, 128), 1), iota((R, 128), 0)
         picked = [
@@ -293,11 +296,10 @@
         own = jnp.dot(jnp.concatenate(picked, axis=0), homes, preferred_element_type=F32)
         for k in (1, 3, 2):
             received(ro2.at[half, k - 1], s2.at[half, 0, 0], r2.at[half, k - 1, 1])
-        parts = [[m1[half, q * 4 + u]] + [ro2[half, k, u] for k in range(3)] for u in range(4)]
+        parts = [[m1[half, u]] + [ro2[half, k, u] for k in range(3)] for u in range(4)]
         for u, result in enumerate(scaled_sums(lent[0:4], parts)):
             att[(half * 4 + u) * R : (half * 4 + u + 1) * R] = result + own[u * R : (u + 1) * R]
 
-    home_part()
     for dp in FORWARD:
         forward(dp)
     c_inv.wait()
@@ -317,6 +319,7 @@
             seen[dp] += 1
         for dp in sorted({dp for dp, _ in pairs if seen[dp] == 4}):
             send_line(dp)
+    home_part()
     lent = sent[GATHER:]
     del sent[GATHER:]
     all_sent()
@@ -402,7 +405,7 @@
             v(4, R, 1024), v(4, R, 1024), v(3, R, 1024), v(3, R, 1024),
             pltpu.SMEM((SLOTS,), I32), pltpu.SMEM((OWN,), I32), v(8, 128, dtype=I32), pltpu.SMEM((8, 128), I32),
             dma((11,)), dma((2,)), dma((2, 15)), dma((2, 4, 4)),
-            dma((2, 3, 2)), dma((2, 3, 2)), dma((2, 3, 2)), dma((2, 3, 2)),
+            dma((2, 3, 3)), dma((2, 3, 3)), dma((2, 3, 2)), dma((2, 3, 2)),
             dma((4,)), dma((4,)), dma((3,)), dma((3,)),
         ],
         name="lent_attention",

time: 38.8 us -> 38.5 us (level)
  Pallas kernels: 38.1 us -> 37.7 us
where the time goes in v4:
time: 38.5 us; the launch traced here: 38.4 us
  Pallas kernels  37.7 us (98%)
  local copies, waits for them, and re-layouts  0.66 us (2%)
    pallas_call x1, Pallas kernels, per_device(): pl.pallas_call(kernel, out_shape=jax.ShapeDtypeStruct((R, 1024), BF16), i...  37.7 us

profile of v4, /device:TPU:1, one launch (start us, length us, event | category | flops | bytes accessed | tf_op | source)
XLA Modules:
  0.0 38.4 jit_solution(11743537989172082938)
XLA Ops:
  0.0 37.7 %lent_attention.1 = bf16[32,1024]{1,0:T(8,128)(2,1)S(1)} custom-call(s32[48]{0:T(128)} %sr_hbm.1, s32[8]{0:T(128)} %tl_hbm.1, bf16[8,32,128]{2,1,0:T(8,128)(2,1)} %bitcast.11, bf16[8,256,128]{2,1,0:T(8,128)(2,1)} %bitcast.9, bf16[8,256,128]{2,1,0:T(8,128)(2,1)} %bitcast.10, bf16[32,128]{1,0:T(8,128)(2,1)} %bitcast.12, bf16[32,128]{1,0:T(8,128)(2,1)} %bitcast.13, ...), custom_call_target="tpu_custom_call" | custom-call | tf_op jit(solution)/shard_map/lent_attention/pallas_call | solution.py:392
  37.8 0.7 %reshape.31 = bf16[8,4,1024]{2,1,0:T(4,128)(2,1)} reshape(bf16[32,1024]{1,0:T(8,128)(2,1)S(1)} %lent_attention.1) | data formatting | bytes 131072 | tf_op jit(solution)/shard_map/reshape | solution.py:414

commit v5 on v4

--- a/solution.py
+++ b/solution.py
@@ -274,14 +274,18 @@
         for k in FIRST:
             for start, end in ((0, EARLY), (EARLY, 16)) if EARLY and k != 2 else ((0, 16),):
                 received(ro1.at[half, k - 1, pl.ds(start, end - start)], s1.at[half, 0, 0], r1.at[half, k - 1, int(start > 0)])
-        for i in range(0, 16, 4):
-            parts = [[omsg[base + i + u]] + [ro1[half, k, i + u] for k in range(3)] for u in range(4)]
-            for u, result in enumerate(scaled_sums(weights[i : i + 4], parts)):
-                m1[half, i + u] = result.astype(BF16)
+
+        def merge(k):
+            parts = [[omsg[base + k * 4 + u]] + [ro1[half, n, k * 4 + u] for n in range(3)] for u in range(4)]
+            for u, result in enumerate(scaled_sums(weights[k * 4 : k * 4 + 4], parts)):
+                m1[half, k * 4 + u] = result.astype(BF16)
+
         for k in (2, 1, 3):
             to = along(half, 1, k)
+            send(l1.at[half, k], rl2.at[half, k - 1], s2.at[half, k - 1, 0], r2.at[half, k - 1, 0], to)
+            merge(k)
             send(m1.at[half, pl.ds(k * 4, 4)], ro2.at[half, k - 1], s2.at[half, k - 1, 1], r2.at[half, k - 1, 1], to)
-            send(l1.at[half, k], rl2.at[half, k - 1], s2.at[half, k - 1, 0], r2.at[half, k - 1, 0], to)
+        return merge
 
     def second_merge(half):
         for k in (1, 3, 2):
@@ -323,8 +327,9 @@
     lent = sent[GATHER:]
     del sent[GATHER:]
     all_sent()
-    for half in (0, 1):
-        first_merge(half)
+    own_merges = [first_merge(half) for half in (0, 1)]
+    for merge in own_merges:
+        merge(0)
     for copy in lent:
         copy.wait_send()
     for half in (0, 1):
@@ -333,21 +338,22 @@
     flat = jnp.concatenate([att[pl.ds(h, R, stride=8)].astype(BF16) for h in range(8)], axis=1)
     c_w.wait()
 
-    def columns(target):
-        return jnp.dot(flat, wb[:, pl.ds(pl.multiple_of(target * 1024, 1024), 1024)], preferred_element_type=F32)
+    def columns(target, start=0, width=1024):
+        at = pl.multiple_of(target * 1024 + start, 512)
+        return jnp.dot(flat, wb[:, pl.ds(at, width)], preferred_element_type=F32)
 
     def share(dy):
         cs[dy] = columns(((y + dy) % 4) * 2 + 1 - c).astype(BF16)
         send(cs.at[dy], cr.at[dy], css.at[dy], crs.at[dy], {"tp": y * 2 + 1 - c})
 
-    def both(dy):
-        value = columns(((y + dy) % 4) * 2 + c)
-        received(cr.at[dy], css.at[dy], crs.at[dy])
-        return value + cr[dy].astype(F32)
-
     def along_y(dy):
-        ys[dy - 1] = both(dy).astype(BF16)
-        send(ys.at[dy - 1], yr.at[dy - 1], yss.at[dy - 1], yrs.at[dy - 1], {"tp": ((y + dy) % 4) * 2 + c})
+        for n in (0, 1):
+            value = columns(((y + dy) % 4) * 2 + c, n * 512, 512)
+            if n == 0:
+                received(cr.at[dy], css.at[dy], crs.at[dy])
+            ys[dy - 1, n] = (value + cr[dy, :, n * 512 : (n + 1) * 512].astype(F32)).astype(BF16)
+            to = {"tp": ((y + dy) % 4) * 2 + c}
+            send(ys.at[dy - 1, n], yr.at[dy - 1, n], yss.at[dy - 1, n], yrs.at[dy - 1, n], to)
 
     share(2)
     share(1)
@@ -356,13 +362,16 @@
     along_y(1)
     along_y(3)
     share(0)
-    value = both(0)
-    last = sent[-4:]
-    del sent[-4:]
+    value = columns(y * 2 + c)
+    received(cr.at[0], css.at[0], crs.at[0])
+    value = value + cr[0].astype(F32)
+    last = sent[-7:]
+    del sent[-7:]
     all_sent()
     for dy in (2, 1, 3):
-        received(yr.at[dy - 1], yss.at[dy - 1], yrs.at[dy - 1])
-        value = value + yr[dy - 1].astype(F32)
+        for n in (0, 1):
+            received(yr.at[dy - 1, n], yss.at[dy - 1, n], yrs.at[dy - 1, n])
+        value = value + jnp.concatenate([yr[dy - 1, 0], yr[dy - 1, 1]], axis=1).astype(F32)
     out[...] = value.astype(BF16)
     for copy in last:
         copy.wait_send()
@@ -402,11 +411,11 @@
             v(2, 16, R, HD), v(2, 4, 8, 128, dtype=F32),
             v(2, 3, 4, R, HD), v(2, 3, 8, 128, dtype=F32),
             v(OWN, R, HD), v(2, 8, 128, dtype=F32), v(OWN * R, HD, dtype=F32),
-            v(4, R, 1024), v(4, R, 1024), v(3, R, 1024), v(3, R, 1024),
+            v(4, R, 1024), v(4, R, 1024), v(3, 2, R, 512), v(3, 2, R, 512),
             pltpu.SMEM((SLOTS,), I32), pltpu.SMEM((OWN,), I32), v(8, 128, dtype=I32), pltpu.SMEM((8, 128), I32),
             dma((11,)), dma((2,)), dma((2, 15)), dma((2, 4, 4)),
             dma((2, 3, 3)), dma((2, 3, 3)), dma((2, 3, 2)), dma((2, 3, 2)),
-            dma((4,)), dma((4,)), dma((3,)), dma((3,)),
+            dma((4,)), dma((4,)), dma((3, 2)), dma((3, 2)),
         ],
         name="lent_attention",
         compiler_params=pltpu.CompilerParams(collective_id=0, has_side_effects=True, vmem_limit_bytes=44 * 2**20),

time: 38.5 us -> 38.3 us (level)
  no operation moved by 1% of the time
where the time goes in v5:
time: 38.3 us; the launch traced here: 38.2 us
  Pallas kernels  37.6 us (98%)
  local copies, waits for them, and re-layouts  0.66 us (2%)
    pallas_call x1, Pallas kernels, per_device(): pl.pallas_call(kernel, out_shape=jax.ShapeDtypeStruct((R, 1024), BF16), i...  37.6 us

profile of v5, /device:TPU:1, one launch (start us, length us, event | category | flops | bytes accessed | tf_op | source)
XLA Modules:
  0.0 38.2 jit_solution(3244581025020722076)
XLA Ops:
  0.0 37.6 %lent_attention.1 = bf16[32,1024]{1,0:T(8,128)(2,1)S(1)} custom-call(s32[48]{0:T(128)} %sr_hbm.1, s32[8]{0:T(128)} %tl_hbm.1, bf16[8,32,128]{2,1,0:T(8,128)(2,1)} %bitcast.11, bf16[8,256,128]{2,1,0:T(8,128)(2,1)} %bitcast.9, bf16[8,256,128]{2,1,0:T(8,128)(2,1)} %bitcast.10, bf16[32,128]{1,0:T(8,128)(2,1)} %bitcast.12, bf16[32,128]{1,0:T(8,128)(2,1)} %bitcast.13, ...), custom_call_target="tpu_custom_call" | custom-call | tf_op jit(solution)/shard_map/lent_attention/pallas_call | solution.py:401
  37.6 0.7 %reshape.31 = bf16[8,4,1024]{2,1,0:T(4,128)(2,1)} reshape(bf16[32,1024]{1,0:T(8,128)(2,1)S(1)} %lent_attention.1) | data formatting | bytes 131072 | tf_op jit(solution)/shard_map/reshape | solution.py:423

commit v6 on v5

--- a/solution.py
+++ b/solution.py
@@ -346,8 +346,8 @@
         cs[dy] = columns(((y + dy) % 4) * 2 + 1 - c).astype(BF16)
         send(cs.at[dy], cr.at[dy], css.at[dy], crs.at[dy], {"tp": y * 2 + 1 - c})
 
-    def along_y(dy):
-        for n in (0, 1):
+    def along_y(*pieces):
+        for dy, n in pieces:
             value = columns(((y + dy) % 4) * 2 + c, n * 512, 512)
             if n == 0:
                 received(cr.at[dy], css.at[dy], crs.at[dy])
@@ -358,9 +358,7 @@
     share(2)
     share(1)
     share(3)
-    along_y(2)
-    along_y(1)
-    along_y(3)
+    along_y((2, 0), (2, 1), (1, 0), (3, 0), (1, 1), (3, 1))
     share(0)
     value = columns(y * 2 + c)
     received(cr.at[0], css.at[0], crs.at[0])

time: 38.3 us -> 38.3 us (level)
  no operation moved by 1% of the time
where the time goes in v6:
time: 38.3 us; the launch traced here: 38.2 us
  Pallas kernels  37.6 us (98%)
  local copies, waits for them, and re-layouts  0.66 us (2%)
    pallas_call x1, Pallas kernels, per_device(): pl.pallas_call(kernel, out_shape=jax.ShapeDtypeStruct((R, 1024), BF16), i...  37.6 us

profile of v6, /device:TPU:1, one launch (start us, length us, event | category | flops | bytes accessed | tf_op | source)
XLA Modules:
  0.0 38.2 jit_solution(11464189168480381260)
XLA Ops:
  0.0 37.6 %lent_attention.1 = bf16[32,1024]{1,0:T(8,128)(2,1)S(1)} custom-call(s32[48]{0:T(128)} %sr_hbm.1, s32[8]{0:T(128)} %tl_hbm.1, bf16[8,32,128]{2,1,0:T(8,128)(2,1)} %bitcast.11, bf16[8,256,128]{2,1,0:T(8,128)(2,1)} %bitcast.9, bf16[8,256,128]{2,1,0:T(8,128)(2,1)} %bitcast.10, bf16[32,128]{1,0:T(8,128)(2,1)} %bitcast.12, bf16[32,128]{1,0:T(8,128)(2,1)} %bitcast.13, ...), custom_call_target="tpu_custom_call" | custom-call | tf_op jit(solution)/shard_map/lent_attention/pallas_call | solution.py:399
  37.6 0.7 %reshape.31 = bf16[8,4,1024]{2,1,0:T(4,128)(2,1)} reshape(bf16[32,1024]{1,0:T(8,128)(2,1)S(1)} %lent_attention.1) | data formatting | bytes 131072 | tf_op jit(solution)/shard_map/reshape | solution.py:421
